TPU v7x, 128 devices: a whole 4x4x4 slice. The times are simulated.
128 devices in a mesh: dp: 64 (over x, z_lo, y, core), tensor: 2 (over z_hi).
Axes of the slice: x: 4, y: 4, z: 4 (z_hi: 2, z_lo: 2; z = z_hi * 2 + z_lo), core: 2. Of those that a mesh axis runs over, the one named last changes fastest.
Arguments:
- inputs: bfloat16 [256, 197, 768], P(('dp', 'tensor')), may hold values from -6 to 6
- image_counts: int32 [64], P('dp'), may hold values from 1 to 4, as said below
- first_gain: float32 [768], replicated, may hold values from 0.5 to 1.5
- first_shift: float32 [768], replicated, may hold values from -1.5 to 1.5
- project_weight: bfloat16 [768, 3, 768], P(None, None, 'tensor'), may hold values from -0.21875 to 0.21875
- project_bias: float32 [2, 768], P(None, 'tensor'), may hold values from -1.5 to 1.5
- output_weight: bfloat16 [768, 768], P('tensor'), may hold values from -0.625 to 0.625
- output_bias: float32 [768], replicated, may hold values from -1.5 to 1.5
- second_gain: float32 [768], replicated, may hold values from 0.5 to 1.5
- second_shift: float32 [768], replicated, may hold values from -1.5 to 1.5
- expand_weight: bfloat16 [768, 3072], P(None, 'tensor'), may hold values from -0.21875 to 0.21875
- expand_bias: float32 [3072], P('tensor'), may hold values from -1.5 to 1.5
- reduce_weight: bfloat16 [3072, 768], P('tensor'), may hold values from -0.109375 to 0.109375
- reduce_bias: float32 [768], replicated, may hold values from -1.5 to 1.5
- out_cotangent: bfloat16 [256, 197, 768], P(('dp', 'tensor')), may hold values from -6 to 6
Outputs:
- block_out: bfloat16 [256, 197, 768], P(('dp', 'tensor'))
- input_grad: float32 [256, 197, 768], P(('dp', 'tensor'))
- grad_first_gain: float32 [768], replicated
- grad_first_shift: float32 [768], replicated
- grad_project_weight: float32 [768, 3, 768], P(None, None, 'tensor')
- grad_project_bias: float32 [2, 768], P(None, 'tensor')
- grad_output_weight: float32 [768, 768], P('tensor')
- grad_output_bias: float32 [768], replicated
- grad_second_gain: float32 [768], replicated
- grad_second_shift: float32 [768], replicated
- grad_expand_weight: float32 [768, 3072], P(None, 'tensor')
- grad_expand_bias: float32 [3072], P('tensor')
- grad_reduce_weight: float32 [3072, 768], P('tensor')
- grad_reduce_bias: float32 [768], replicated
Inputs may be any that keep to these rules, and one draw needn't show every extreme that they name: image_counts[i] live images fill the first slots of dp device i's 4; the rest are padding; in every draw some device is full.
All inputs are finite; a program needn't handle non-finite values.
Results may differ from a plain program's by a relative error of at most 0.014.
Values may be sent and summed in bfloat16 or wider, within the bound.
A program may use at most 192 MiB of HBM per device.

v0:
```python
import jax
import jax.numpy as jnp
from jax import lax
from jax.sharding import PartitionSpec as P

HD = 64


EPSILON = 1e-06


def joined_along(blocks, dim):
    dims = list(blocks.shape[1:])
    dims[dim] *= blocks.shape[0]
    return jnp.moveaxis(blocks, 0, dim).reshape(dims)


def copy_for_each(shard, axis):
    length = lax.axis_size(axis)
    return lax.all_to_all(
        jnp.broadcast_to(shard[None], (length, *shard.shape)), axis, 0, 0, tiled=True
    )


def gathered_copies(shard, axis, dim):
    return joined_along(copy_for_each(shard, axis), dim)


def in_blocks(shard, dim, length):
    dims = shard.shape
    blocks = shard.reshape(*dims[:dim], length, dims[dim] // length, *dims[dim + 1 :])
    return jnp.moveaxis(blocks, dim, 0)


def sum_at_owner(shard, axis, dim):
    blocks = in_blocks(shard, dim, lax.axis_size(axis))
    arrived = lax.all_to_all(blocks, axis, split_axis=0, concat_axis=0, tiled=True)
    return arrived.sum(axis=0)


def sum_at_owner_2(shard, axis, dim):
    blocks = in_blocks(shard, dim, lax.axis_size(axis))
    arrived = lax.all_to_all(blocks, axis, split_axis=0, concat_axis=0, tiled=True)
    return arrived.astype(jnp.float32).sum(axis=0)


def layer_norm(stream, gain, shift):
    center = jnp.mean(stream, axis=-1, keepdims=True)
    centered = stream - center
    spread = jnp.mean(centered * centered, axis=-1, keepdims=True)
    return centered * lax.rsqrt(spread + EPSILON) * gain + shift


def column_sum(matrix):
    return jnp.dot(
        jnp.ones((matrix.shape[0],), jnp.bfloat16), matrix, preferred_element_type=jnp.float32
    )


def gelu_exact(entry):
    return jax.nn.gelu(entry, approximate=False)


def shards(
    inputs,
    image_counts,
    first_gain,
    first_shift,
    project_weight,
    project_bias,
    output_weight,
    output_bias,
    second_gain,
    second_shift,
    expand_weight,
    expand_bias,
    reduce_weight,
    reduce_bias,
    out_cotangent,
):
    half_slots, tokens_image, model_width = inputs.shape
    local_width = project_weight.shape[2]
    local_heads = local_width // HD
    all_slots = half_slots * lax.axis_size("tensor")
    slot_ids = lax.axis_index("tensor") * half_slots + jnp.arange(half_slots, dtype=jnp.int32)
    keeping = (slot_ids < image_counts[0]).astype(jnp.float32)[:, None, None]
    score_scale = HD ** (-0.5)
    flat_project = project_weight.reshape(model_width, 3 * local_width)
    head_shape = (all_slots, tokens_image, local_heads, HD)
    stream = inputs.astype(jnp.float32)
    normed_all = gathered_copies(
        layer_norm(stream, first_gain, first_shift).astype(jnp.bfloat16), "tensor", 0
    )
    flat_normed = normed_all.reshape(-1, model_width)
    projected = jnp.dot(flat_normed, flat_project, preferred_element_type=jnp.float32).reshape(
        all_slots, tokens_image, 3, local_width
    )
    queries = (projected[:, :, 0] + project_bias[0]).astype(jnp.bfloat16).reshape(head_shape)
    key_rows = projected[:, :, 1].astype(jnp.bfloat16).reshape(head_shape)
    values = (projected[:, :, 2] + project_bias[1]).astype(jnp.bfloat16).reshape(head_shape)
    scores = (
        jnp.einsum("bqhd,bkhd->bhqk", queries, key_rows, preferred_element_type=jnp.float32)
        * score_scale
    )
    row_max = jnp.max(scores, axis=-1, keepdims=True)
    raised = jnp.exp(scores - row_max)
    row_total = jnp.sum(raised, axis=-1, keepdims=True)
    log_total = row_max + jnp.log(row_total)
    soft_low = (raised / row_total).astype(jnp.bfloat16)
    head_mixed = (
        jnp.einsum("bhqk,bkhd->bqhd", soft_low, values, preferred_element_type=jnp.float32)
        .reshape(all_slots, tokens_image, local_width)
        .astype(jnp.bfloat16)
    )
    picked = head_mixed
    resid = (
        stream
        + sum_at_owner(
            jnp.einsum("bsh,hd->bsd", picked, output_weight, preferred_element_type=jnp.float32),
            "tensor",
            0,
        )
        + output_bias
    )
    normed_two = gathered_copies(
        layer_norm(resid, second_gain, second_shift).astype(jnp.bfloat16), "tensor", 0
    ).reshape(-1, model_width)
    hidden = jnp.dot(normed_two, expand_weight, preferred_element_type=jnp.float32) + expand_bias
    active = gelu_exact(hidden).astype(jnp.bfloat16)
    picked = active
    branch = sum_at_owner_2(
        jnp.dot(picked, reduce_weight, preferred_element_type=jnp.float32)
        .reshape(half_slots * lax.axis_size("tensor"), tokens_image, model_width)
        .astype(jnp.bfloat16),
        "tensor",
        0,
    )
    block_out = ((resid + branch + reduce_bias) * keeping).astype(jnp.bfloat16)
    grad_out = out_cotangent.astype(jnp.float32) * keeping
    grad_rows = gathered_copies(grad_out.astype(jnp.bfloat16), "tensor", 0).reshape(-1, model_width)
    grad_reduce_weight = jnp.einsum(
        "rf,rd->fd", active, grad_rows, preferred_element_type=jnp.float32
    )
    grad_reduce_bias = column_sum(grad_rows)
    grad_active = jnp.einsum(
        "rd,fd->rf", grad_rows, reduce_weight, preferred_element_type=jnp.float32
    )
    gelu_pull = jax.vjp(gelu_exact, hidden)[1]
    grad_hidden = gelu_pull(grad_active)[0].astype(jnp.bfloat16)
    grad_expand_weight = jnp.einsum(
        "rd,rf->df", normed_two, grad_hidden, preferred_element_type=jnp.float32
    )
    grad_expand_bias = column_sum(grad_hidden)
    feed_sums = (grad_expand_weight, grad_expand_bias, grad_reduce_weight, grad_reduce_bias)
    feed_sums = lax.psum(
        (grad_expand_weight, grad_expand_bias, grad_reduce_weight, grad_reduce_bias), "dp"
    )
    picked = grad_hidden
    grad_normed_two = sum_at_owner_2(
        jnp.einsum("rf,df->rd", picked, expand_weight, preferred_element_type=jnp.float32)
        .reshape(half_slots * lax.axis_size("tensor"), tokens_image, model_width)
        .astype(jnp.bfloat16),
        "tensor",
        0,
    )
    norm_two_pull = jax.vjp(layer_norm, resid, second_gain, second_shift)[1]
    grad_resid_norm, grad_second_gain, grad_second_shift = norm_two_pull(grad_normed_two)
    grad_resid = grad_out + grad_resid_norm
    grad_attended = gathered_copies(grad_resid.astype(jnp.bfloat16), "tensor", 0).reshape(
        -1, model_width
    )
    grad_output_weight = jnp.einsum(
        "rh,rd->hd",
        head_mixed.reshape(-1, local_width),
        grad_attended,
        preferred_element_type=jnp.float32,
    )
    grad_output_bias = column_sum(grad_attended)
    grad_mixed = (
        jnp.einsum("rd,hd->rh", grad_attended, output_weight, preferred_element_type=jnp.float32)
        .astype(jnp.bfloat16)
        .reshape(head_shape)
    )
    soft_again = jnp.exp(
        jnp.einsum("bqhd,bkhd->bhqk", queries, key_rows, preferred_element_type=jnp.float32)
        * score_scale
        - log_total
    )
    grad_values = jnp.einsum(
        "bhqk,bqhd->bkhd",
        soft_again.astype(jnp.bfloat16),
        grad_mixed,
        preferred_element_type=jnp.float32,
    ).astype(jnp.bfloat16)
    grad_soft = jnp.einsum(
        "bqhd,bkhd->bhqk", grad_mixed, values, preferred_element_type=jnp.float32
    )
    inner_sum = jnp.sum(soft_again * grad_soft, axis=-1, keepdims=True)
    grad_scores = (soft_again * (grad_soft - inner_sum)).astype(jnp.bfloat16)
    grad_queries = (
        jnp.einsum("bhqk,bkhd->bqhd", grad_scores, key_rows, preferred_element_type=jnp.float32)
        * score_scale
    ).astype(jnp.bfloat16)
    grad_keys = (
        jnp.einsum("bhqk,bqhd->bkhd", grad_scores, queries, preferred_element_type=jnp.float32)
        * score_scale
    ).astype(jnp.bfloat16)
    grad_projected = jnp.stack([grad_queries, grad_keys, grad_values], axis=2).reshape(
        -1, 3 * local_width
    )
    grad_project_weight = jnp.einsum(
        "rd,rc->dc", flat_normed, grad_projected, preferred_element_type=jnp.float32
    ).reshape(model_width, 3, local_width)
    bias_sums = column_sum(grad_projected).reshape(3, local_width)
    grad_project_bias = jnp.stack([bias_sums[0], bias_sums[2]])
    picked = grad_projected
    grad_normed_one = sum_at_owner_2(
        jnp.einsum("rc,dc->rd", picked, flat_project, preferred_element_type=jnp.float32)
        .reshape(half_slots * lax.axis_size("tensor"), tokens_image, model_width)
        .astype(jnp.bfloat16),
        "tensor",
        0,
    )
    norm_one_pull = jax.vjp(layer_norm, stream, first_gain, first_shift)[1]
    grad_stream_norm, grad_first_gain, grad_first_shift = norm_one_pull(grad_normed_one)
    input_grad = grad_resid + grad_stream_norm
    norm_sums = lax.psum(
        (grad_first_gain, grad_first_shift, grad_second_gain, grad_second_shift), ("dp", "tensor")
    )
    attend_sums = lax.psum(
        (grad_project_weight, grad_project_bias, grad_output_weight, grad_output_bias), "dp"
    )
    summed = attend_sums + feed_sums
    return (
        block_out,
        input_grad,
        norm_sums[0],
        norm_sums[1],
        summed[0],
        summed[1],
        summed[2],
        summed[3],
        norm_sums[2],
        norm_sums[3],
        summed[4],
        summed[5],
        summed[6],
        summed[7],
    )


def solution(mesh):
    in_specs = (
        P(("dp", "tensor"), None, None),
        P("dp"),
        P(),
        P(),
        P(None, None, "tensor"),
        P(None, "tensor"),
        P("tensor", None),
        P(),
        P(),
        P(),
        P(None, "tensor"),
        P("tensor"),
        P("tensor", None),
        P(),
        P(("dp", "tensor"), None, None),
    )
    out_specs = (
        P(("dp", "tensor"), None, None),
        P(("dp", "tensor"), None, None),
        P(),
        P(),
        P(None, None, "tensor"),
        P(None, "tensor"),
        P("tensor", None),
        P(),
        P(),
        P(),
        P(None, "tensor"),
        P("tensor"),
        P("tensor", None),
        P(),
    )
    return jax.shard_map(shards, mesh=mesh, in_specs=in_specs, out_specs=out_specs, check_vma=False)
```

profile of v0, /device:TPU:1, one launch (start us, length us, event | category | flops | bytes accessed | tf_op | source)
XLA Modules:
  0.0 875.3 jit_solution(8457967068008119735)
XLA Ops:
  14.3 5.8 all-to-all-start
  20.9 3.8 copy.70
  24.8 11.9 %all-to-all-done = bf16[2,2,197,768]{3,1,2,0:T(2,128)(2,1)} async-done(((bf16[2,2,197,768]{3,1,2,0:T(2,128)(2,1)}), bf16[2,2,197,768]{3,1,2,0:T(2,128)(2,1)}, u32[]{:S(2)}, u32[]{:S(2)}) %all-to-all-start) | async-done | bytes 1210400 | tf_op jit(solution)/shard_map/all_to_all | solution.py:20
  61.1 5.1 all-to-all-start.1
  70.0 24.5 %all-to-all-done.1 = f32[2,2,197,768]{3,1,2,0:T(2,128)} async-done(((f32[2,2,197,768]{3,1,2,0:T(2,128)}), f32[2,2,197,768]{3,1,2,0:T(2,128)}, u32[]{:S(2)}, u32[]{:S(2)}) %all-to-all-start.1) | async-done | bytes 2420768 | tf_op jit(solution)/shard_map/all_to_all | solution.py:37
  97.2 4.5 all-to-all-start.4
  101.7 4.5 reduce_sum.162
  110.9 5.2 all-to-all-done.4
  118.8 4.5 all-to-all-start.2
  142.9 4.2 fusion.64
  147.1 14.1 %add_convert_fusion = (bf16[788,1536]{1,0:T(8,128)(2,1)S(1)}, f32[788,1536]{1,0:T(8,128)}) fusion(f32[788,1536]{1,0:T(8,128)S(1)} %fusion.64, f32[1536]{0:T(1024)S(1)} %copy-done.63, bf16[788,768]{1,0:T(8,128)(2,1)S(1)} %copy-done.18, bf16[1536,768]{1,0:T(8,128)(2,1)S(1)} %copy-done), kind=kOutput, calls=%fused_computation.7 | convolution fusion | flops 1947482112 | bytes 15679488 | tf_op jit(solution)/shard_map/rd,fd->rf/dot_general | solution.py:145
  171.6 4.9 all-to-all-start.5
  176.5 6.5 multiply_convert_fusion.1
  183.0 6.7 all-to-all-done.5
  189.7 4.1 convert_reduce_fusion.2
  198.4 4.5 all-to-all-start.6
  202.9 7.0 fusion.67
  210.0 4.5 fusion.68
  228.9 3.8 fusion.27
  232.7 4.4 multiply_reduce_fusion
  248.5 5.6 reshape.172
  254.1 6.0 fusion.65
  260.1 4.8 convolution_convert_fusion.2
  270.8 4.5 all-to-all-start.3
  279.0 14.8 %all-to-all-done.3 = bf16[2,2,197,768]{3,1,2,0:T(2,128)(2,1)} async-done(((bf16[2,2,197,768]{3,1,2,0:T(2,128)(2,1)}), bf16[2,2,197,768]{3,1,2,0:T(2,128)(2,1)}, u32[]{:S(2)}, u32[]{:S(2)}) %all-to-all-start.3) | async-done | bytes 1210400 | tf_op jit(solution)/shard_map/all_to_all | solution.py:43
  293.9 4.5 convert_reduce_fusion.4
  303.6 4.5 all-to-all-start.7
  310.8 275.4 %all-reduce.1 = (f32[2,384]{1,0:T(2,128)}, f32[768]{0:T(1024)}, f32[1536]{0:T(1024)}, f32[768]{0:T(1024)}) all-reduce(f32[2,384]{1,0:T(2,128)S(1)} %pad_maximum_fusion.1, f32[768]{0:T(1024)S(1)} %convolution_reduce_fusion.3, f32[1536]{0:T(1024)S(1)} %convolution_reduce_fusion, ...), channel_id=1, replica_groups=mesh['dp'=64,'tensor'=2] {'dp'}, use_global_device_ids=true, to_apply=%region_20.0 | all-reduce | flops 3840 | bytes 30720 | tf_op jit(solution)/shard_map/psum | solution.py:230
  586.2 3.9 convert_reduce_fusion
  596.2 70.7 %all-reduce = (f32[768]{0:T(1024)}, f32[768]{0:T(1024)}, f32[768]{0:T(1024)}, f32[768]{0:T(1024)}) all-reduce(f32[768]{0:T(1024)S(1)} %get-tuple-element.30, f32[768]{0:T(1024)S(1)} %get-tuple-element.34, f32[768]{0:T(1024)S(1)} %copy-done.62, f32[768]{0:T(1024)S(1)} %copy-done.61), channel_id=1, replica_groups=mesh['dp'=64,'tensor'=2] {'dp','tensor'}, use_global_device_ids=true, to_apply=%region_16.0 | all-reduce | flops 3072 | bytes 24576 | tf_op jit(solution)/shard_map/psum | solution.py:227
  666.9 190.3 %all-reduce.5.cloned.1.call-done = (f32[768,3,384]{2,0,1:T(8,128)}, f32[384,768]{1,0:T(8,128)}, f32[768,1536]{1,0:T(8,128)}, f32[1536,768]{1,0:T(8,128)}) async-done(((f32[768,3,384]{2,0,1:T(8,128)}, f32[384,768]{1,0:T(8,128)}, f32[768,1536]{1,0:T(8,128)}, f32[1536,768]{1,0:T(8,128)}), (f32[768,3,384]{2,0,1:T(8,128)}, f32[384,768]{1,0:T(8,128)}, f32[768,1536]{1,0:T(8,128)}, ...) | async-done | bytes 14155792 | tf_op jit(solution)/shard_map/psum | solution.py:230
  857.2 4.2 copy.171
  (242 shorter events, 135.6 us)
Async XLA Ops:
  7.2 139.9 %copy-start = (bf16[1536,768]{1,0:T(8,128)(2,1)S(1)}, bf16[1536,768]{1,0:T(8,128)(2,1)}, u32[]{:S(2)}) copy-start(bf16[1536,768]{1,0:T(8,128)(2,1)} %param.27) | copy-start | bytes 7077892
  14.3 5.8 copy-start.69
  14.3 22.3 %all-to-all-start = ((bf16[2,2,197,768]{3,1,2,0:T(2,128)(2,1)}), bf16[2,2,197,768]{3,1,2,0:T(2,128)(2,1)}, u32[]{:S(2)}, u32[]{:S(2)}) async-start(bf16[2,2,197,768]{3,1,2,0:T(2,128)(2,1)} %broadcast_in_dim.16), calls=%async_computation | async-start | bytes 2420736 | tf_op jit(solution)/shard_map/all_to_all | solution.py:20
  20.9 30.1 %copy-start.47 = (f32[6,64]{1,0:T(8,128)}, f32[6,64]{1,0:T(8,128)S(1)}, u32[]{:S(2)}) copy-start(f32[6,64]{1,0:T(8,128)S(1)} %add.144) | copy-start | bytes 4612
  61.1 33.4 %all-to-all-start.1 = ((f32[2,2,197,768]{3,1,2,0:T(2,128)}), f32[2,2,197,768]{3,1,2,0:T(2,128)}, u32[]{:S(2)}, u32[]{:S(2)}) async-start(f32[2,2,197,768]{3,1,2,0:T(2,128)} %copy.76), calls=%async_computation.1 | async-start | bytes 4841472 | tf_op jit(solution)/shard_map/all_to_all | solution.py:37
  97.2 18.9 %all-to-all-start.4 = ((bf16[2,2,197,768]{3,1,2,0:T(2,128)(2,1)}), bf16[2,2,197,768]{3,1,2,0:T(2,128)(2,1)}, u32[]{:S(2)}, u32[]{:S(2)}) async-start(bf16[2,2,197,768]{3,1,2,0:T(2,128)(2,1)} %broadcast_in_dim.18), calls=%async_computation.4 | async-start | bytes 2420736 | tf_op jit(solution)/shard_map/all_to_all | solution.py:20
  118.8 19.0 %all-to-all-start.2 = ((bf16[2,2,197,768]{3,1,2,0:T(2,128)(2,1)}), bf16[2,2,197,768]{3,1,2,0:T(2,128)(2,1)}, u32[]{:S(2)}, u32[]{:S(2)}) async-start(bf16[2,2,197,768]{3,1,2,0:T(2,128)(2,1)} %broadcast_in_dim.17), calls=%async_computation.2 | async-start | bytes 2420736 | tf_op jit(solution)/shard_map/all_to_all | solution.py:20
  142.9 4.2 copy-start.18
  142.9 4.2 copy-start.63
  147.1 14.1 %copy-start.22 = (f32[788,1536]{1,0:T(8,128)}, f32[788,1536]{1,0:T(8,128)S(1)}, u32[]{:S(2)}) copy-start(f32[788,1536]{1,0:T(8,128)S(1)} %fusion.64) | copy-start | bytes 14524420
  147.1 15.5 %copy-start.70 = (bf16[768,1536]{1,0:T(8,128)(2,1)S(1)}, bf16[768,1536]{1,0:T(8,128)(2,1)}, u32[]{:S(2)}) copy-start(bf16[768,1536]{1,0:T(8,128)(2,1)} %param.25) | copy-start | bytes 7077892
  171.6 18.1 %all-to-all-start.5 = ((bf16[2,2,197,768]{3,1,2,0:T(2,128)(2,1)}), bf16[2,2,197,768]{3,1,2,0:T(2,128)(2,1)}, u32[]{:S(2)}, u32[]{:S(2)}) async-start(bf16[2,2,197,768]{3,1,2,0:T(2,128)(2,1)} %copy.85), calls=%async_computation.5 | async-start | bytes 2420736 | tf_op jit(solution)/shard_map/all_to_all | solution.py:43
  189.7 4.1 copy-start.3
  189.7 4.1 copy-start.36
  189.7 4.1 copy-start.39
  198.4 16.7 %all-to-all-start.6 = ((bf16[2,2,197,768]{3,1,2,0:T(2,128)(2,1)}), bf16[2,2,197,768]{3,1,2,0:T(2,128)(2,1)}, u32[]{:S(2)}, u32[]{:S(2)}) async-start(bf16[2,2,197,768]{3,1,2,0:T(2,128)(2,1)} %broadcast_in_dim.21), calls=%async_computation.6 | async-start | bytes 2420736 | tf_op jit(solution)/shard_map/all_to_all | solution.py:20
  202.9 654.3 %all-reduce.5.cloned.1.call-start = ((), (), s32[]{:S(2)}) async-start(), calls=%async_computation.8 | async-start | bytes 28311552 | tf_op jit(solution)/shard_map/psum | solution.py:230
  202.9 7.1 copy-start.19
  202.9 7.1 copy-start.26
  228.9 8.3 slice-start
  232.7 4.5 slice-start.1
  270.8 23.1 %all-to-all-start.3 = ((bf16[2,2,197,768]{3,1,2,0:T(2,128)(2,1)}), bf16[2,2,197,768]{3,1,2,0:T(2,128)(2,1)}, u32[]{:S(2)}, u32[]{:S(2)}) async-start(bf16[2,2,197,768]{3,1,2,0:T(2,128)(2,1)} %copy.80), calls=%async_computation.3 | async-start | bytes 2420736 | tf_op jit(solution)/shard_map/all_to_all | solution.py:43
  293.9 4.5 copy-start.9
  303.6 282.6 %all-to-all-start.7 = ((bf16[2,2,197,768]{3,1,2,0:T(2,128)(2,1)}), bf16[2,2,197,768]{3,1,2,0:T(2,128)(2,1)}, u32[]{:S(2)}, u32[]{:S(2)}) async-start(bf16[2,2,197,768]{3,1,2,0:T(2,128)(2,1)} %copy.98), calls=%async_computation.7 | async-start | bytes 2420736 | tf_op jit(solution)/shard_map/all_to_all | solution.py:43
  310.5 279.6 %copy-start.42 = (f32[2,197]{1,0:T(2,128)S(1)}, f32[2,197]{1,0:T(2,128)}, u32[]{:S(2)}) copy-start(f32[2,197]{1,0:T(2,128)} %copy-done.41) | copy-start | bytes 4732
  310.5 279.6 %copy-start.43 = (f32[768]{0:T(1024)S(1)}, f32[768]{0:T(1024)}, u32[]{:S(2)}) copy-start(f32[768]{0:T(1024)} %param.17) | copy-start | bytes 9220
  586.2 4.4 copy-start.56
  586.2 4.5 copy-start.50
  586.2 5.1 copy-start.23
  857.2 4.2 copy-start.29
  857.2 5.2 copy-start.24
  861.4 4.2 slice-start.2
  (52 other events, 94.6 us)
Sparse Core Ops, SparseCore 0:
  260.2 596.9 all-reduce.4
where the time goes:
time: 885 us; the launch traced here: 875 us
  blocking collectives  346 us (39%)
  waiting for transfers between devices  254 us (29%)
  local copies, waits for them, and re-layouts  109 us (12%)
  matrix products  72.9 us (8%)
  other arithmetic  38.7 us (4%)
  starting transfers between devices  38.3 us (4%)
  between operations  16 us (2%)
    psum x1, blocking collectives, shards(): lax.psum((grad_project_weight, grad_project_bias, grad_output_weight, gra...  275 us
    psum x1, waiting for transfers between devices, shards(): lax.psum((grad_project_weight, grad_project_bias, grad_output_weight, gra...  190 us
    psum x1, blocking collectives, shards(): lax.psum((grad_first_gain, grad_first_shift, grad_second_gain, grad_secon...  70.7 us
    unnamed x157, local copies, waits for them, and re-layouts  29.5 us
    all_to_all x1, waiting for transfers between devices, sum_at_owner(): lax.all_to_all(blocks, axis, split_axis=0, concat_axis=0, tiled=True)  24.5 us
    all_to_all x3, waiting for transfers between devices, sum_at_owner_2(): lax.all_to_all(blocks, axis, split_axis=0, concat_axis=0, tiled=True)  21.5 us
    all_to_all x4, starting transfers between devices, copy_for_each(): lax.all_to_all(jnp.broadcast_to(shard[None], (length, *shard.shape)), axi...  19.2 us
    all_to_all x4, waiting for transfers between devices, copy_for_each(): lax.all_to_all(jnp.broadcast_to(shard[None], (length, *shard.shape)), axi...  17.8 us
  transfers between devices with their start and end apart: 9, of which 7 were waited for; matrix products, arithmetic and copies ran while one was open for 9% of the time, Pallas kernels for 0%

commit v1 on v0

v1 whole, which is shorter than its diff:
```python
import functools

import jax
import jax.numpy as jnp
from jax import lax
from jax.experimental import pallas as pl
from jax.experimental.pallas import tpu as pltpu
from jax.sharding import PartitionSpec as P

HD = 64
EPSILON = 1e-06
TOKENS = 197
ROWS = 208
BOTH = 2 * ROWS
WIDTH = 768
HALF = 384
PAIRS = 6
BLOCK = 48
MESH = pl.DeviceIdType.MESH
F32 = jnp.float32
BF16 = jnp.bfloat16
ANY = pl.BlockSpec(memory_space=pl.ANY)
VMEM = pl.BlockSpec(memory_space=pltpu.VMEM)
SMEM = pl.BlockSpec(memory_space=pltpu.SMEM)


class Place:
    def __init__(self):
        dp = lax.axis_index("dp")
        self.dp = dp
        self.t = lax.axis_index("tensor")
        self.c = lax.rem(dp, 2)
        self.y = lax.rem(lax.div(dp, 2), 4)
        self.zl = lax.rem(lax.div(dp, 8), 2)
        self.x = lax.div(dp, 16)
        self.z = self.t * 2 + self.zl

    def at(self, x=None, y=None, z=None, c=None):
        x = self.x if x is None else x
        y = self.y if y is None else y
        z = self.z if z is None else z
        c = self.c if c is None else c
        return (((x * 2 + lax.rem(z, 2)) * 4 + y) * 2 + c, lax.div(z, 2))

    def neighbours(self):
        return [
            self.at(c=1 - self.c),
            self.at(x=up(self.x)),
            self.at(x=down(self.x)),
            self.at(y=up(self.y)),
            self.at(y=down(self.y)),
            self.at(z=up(self.z)),
            self.at(z=down(self.z)),
        ]


def up(v):
    return lax.rem(v + 1, 4)


def down(v):
    return lax.rem(v + 3, 4)


def across(v):
    return lax.rem(v + 2, 4)


class Post:
    def __init__(self, send_sems, recv_sems):
        self.send_sems, self.recv_sems, self.copies = send_sems, recv_sems, []

    def describe(self, src, dst, device, k):
        return pltpu.make_async_remote_copy(
            src_ref=src,
            dst_ref=dst,
            send_sem=self.send_sems.at[k],
            recv_sem=self.recv_sems.at[k],
            device_id=device,
            device_id_type=MESH,
        )

    def send(self, src, dst, device):
        copy = self.describe(src, dst, device, len(self.copies))
        copy.start()
        self.copies.append(copy)
        return copy

    def drain(self):
        for copy in self.copies:
            copy.wait_send()


def greet(devices):
    barrier = pltpu.get_barrier_semaphore()
    for device in devices:
        pl.semaphore_signal(barrier, inc=1, device_id=device, device_id_type=MESH)
    pl.semaphore_wait(barrier, len(devices))


def gather_blocks(me, post, out):
    x, y, zl, c = me.x, me.y, me.zl, me.c
    xr, xl, xo = up(x), down(x), across(x)
    yr, yl, yo = up(y), down(y), across(y)
    zo = 1 - zl
    to_xr, to_xl = me.at(x=xr), me.at(x=xl)
    to_yr, to_yl = me.at(y=yr), me.at(y=yl)
    to_z = me.at(z=me.t * 2 + zo)
    to_c = me.at(c=1 - c)

    def put(ref, device):
        return post.send(ref, ref, device)

    a, b, d = out.at[0], out.at[1], out.at[2]
    own_a, own_b, own_d = a.at[x, zl, y, c], b.at[x, zl, y, c], d.at[x, zl, y, c]
    a1 = put(own_a, to_z)
    b1r, b1l = put(own_b, to_xr), put(own_b, to_xl)
    d1r, d1l = put(own_d, to_yr), put(own_d, to_yl)
    b1r.wait_recv()
    b1f = put(b.at[xl, zl, y, c], to_xr)
    d1l.wait_recv()
    d1f = put(d.at[x, zl, yr, c], to_yl)
    a1.wait_recv()
    row_a = a.at[x, :, y, c]
    a2r, a2l = put(row_a, to_yr), put(row_a, to_yl)
    b1l.wait_recv()
    b1f.wait_recv()
    b2 = put(b.at[:, zl, y, c], to_z)
    d1r.wait_recv()
    d1f.wait_recv()
    row_d = d.at[x, zl, :, c]
    d2r, d2l = put(row_d, to_xr), put(row_d, to_xl)
    d3 = [put(row_d, to_z)]
    dc = [put(row_d, to_c)]
    a2r.wait_recv()
    a2fr = put(a.at[x, 0, yl, c], to_yr)
    a2l.wait_recv()
    a2fl = put(a.at[x, 1, yr, c], to_yl)
    b2.wait_recv()
    row_b = b.at[:, :, y, c]
    b3r, b3l = put(row_b, to_yr), put(row_b, to_yl)
    bc = [put(row_b, to_c)]
    a2fr.wait_recv()
    a2fl.wait_recv()
    row_a = a.at[x, :, :, c]
    a3r, a3l = put(row_a, to_xr), put(row_a, to_xl)
    ac = [put(row_a, to_c)]
    d2r.wait_recv()
    d2fr = put(d.at[xl, zl, 0:2, c], to_xr)
    d2l.wait_recv()
    d2fl = put(d.at[xr, zl, 2:4, c], to_xl)
    d3.append(put(d.at[xl, zl, :, c], to_z))
    dc.append(put(d.at[xl, zl, :, c], to_c))
    d3.append(put(d.at[xr, zl, :, c], to_z))
    dc.append(put(d.at[xr, zl, :, c], to_c))
    d2fr.wait_recv()
    d2fl.wait_recv()
    d3.append(put(d.at[xo, zl, :, c], to_z))
    dc.append(put(d.at[xo, zl, :, c], to_c))
    b3r.wait_recv()
    b3fr = put(b.at[:, 0, yl, c], to_yr)
    bc.append(put(b.at[:, :, yl, c], to_c))
    b3l.wait_recv()
    b3fl = put(b.at[:, 1, yr, c], to_yl)
    bc.append(put(b.at[:, :, yr, c], to_c))
    a3r.wait_recv()
    a3fr = put(a.at[xl, 0, :, c], to_xr)
    ac.append(put(a.at[xl, :, :, c], to_c))
    a3l.wait_recv()
    a3fl = put(a.at[xr, 1, :, c], to_xl)
    ac.append(put(a.at[xr, :, :, c], to_c))
    for copy, xs in zip(d3, (x, xl, xr, xo)):
        copy.wait_recv()
        dc.append(put(d.at[xs, zo, :, c], to_c))
    a3fr.wait_recv()
    a3fl.wait_recv()
    ac.append(put(a.at[xo, :, :, c], to_c))
    b3fr.wait_recv()
    b3fl.wait_recv()
    bc.append(put(b.at[:, :, yo, c], to_c))
    for copy in ac + bc + dc:
        copy.wait_recv()


GATHER_COPIES = 5 + 2 + 2 + 1 + 2 + 2 + 2 + 2 + 2 + 4 + 2 + 2 + 4 + 4 + 8


def weights_kernel(project, output, expand, reduce, small, out, small_out, send_sems, recv_sems):
    me = Place()
    partner = me.at(z=across(me.z))
    greet(me.neighbours() + [partner])
    post = Post(send_sems, recv_sems)
    dp = me.dp
    place = (me.x, me.zl, me.y, me.c)
    slots = [out.at[(part, *place)] for part in range(3)]

    copies = [post.describe(slots[0], slots[0], partner, 0)]
    post.copies.append(copies[0])

    @pl.when(dp < 48)
    def _():
        rows = pl.multiple_of(lax.rem(dp, 16) * BLOCK, BLOCK)
        post.describe(
            project.at[lax.div(dp, 16), pl.ds(rows, BLOCK), :], slots[0], partner, 0
        ).start()

    @pl.when(dp >= 48)
    def _():
        spot = dp - 48
        rows = pl.multiple_of(lax.rem(spot, 8) * BLOCK, BLOCK)
        cols = pl.multiple_of(lax.div(spot, 8) * HALF, HALF)
        post.describe(
            output.at[pl.ds(rows, BLOCK), pl.ds(cols, HALF)], slots[0], partner, 0
        ).start()

    rows = pl.multiple_of(lax.rem(dp, 16) * BLOCK, BLOCK)
    cols = pl.multiple_of(lax.div(dp, 16) * HALF, HALF)
    copies.append(post.send(expand.at[pl.ds(rows, BLOCK), pl.ds(cols, HALF)], slots[1], partner))
    rows = pl.multiple_of(lax.rem(dp, 32) * BLOCK, BLOCK)
    cols = pl.multiple_of(lax.div(dp, 32) * HALF, HALF)
    copies.append(post.send(reduce.at[pl.ds(rows, BLOCK), pl.ds(cols, HALF)], slots[2], partner))
    small_copy = post.send(small, small_out, partner)
    for copy in copies:
        copy.wait_recv()
    gather_blocks(me, post, out)
    small_copy.wait_recv()
    post.drain()


def other_weights(project, output, expand, reduce, small):
    count = GATHER_COPIES + 4
    return pl.pallas_call(
        weights_kernel,
        out_shape=(
            jax.ShapeDtypeStruct((3, 4, 2, 4, 2, BLOCK, HALF), BF16),
            jax.ShapeDtypeStruct(small.shape, F32),
        ),
        in_specs=[ANY] * 4 + [VMEM],
        out_specs=(ANY, VMEM),
        scratch_shapes=[pltpu.SemaphoreType.DMA((count,)), pltpu.SemaphoreType.DMA((count,))],
        compiler_params=pltpu.CompilerParams(collective_id=0, has_side_effects=True),
        name="weights_gather",
    )(project, output, expand, reduce, small)


def add_blocks(count, target, sources):
    def step(k, carry):
        ref = target(k)
        total = ref[...].astype(F32)
        for source in sources:
            total = total + source(k)[...].astype(F32)
        ref[...] = total.astype(BF16)
        return carry

    lax.fori_loop(0, count, step, 0)


class Ring:
    def __init__(self, post, me, right, left, view, blocks, block_of, bufs):
        self.post, self.me, self.right, self.left = post, me, right, left
        self.view, self.blocks, self.block_of = view, blocks, block_of
        self.relay_l, self.relay_r, self.left_a, self.left_b, self.right_a, self.right_b = bufs

    def add(self, half, d, bufs):
        ref = self.view(half, d)
        if self.blocks[half] is None:
            total = ref[...].astype(F32)
            for buf in bufs:
                total = total + buf[...].astype(F32)
            ref[...] = total.astype(BF16)
        else:
            add_blocks(
                self.blocks[half],
                lambda k: self.block_of(ref, k),
                [lambda k, buf=buf: self.block_of(buf, k) for buf in bufs],
            )

    def start_far(self):
        far = across(self.me)
        self.far_r = self.post.send(self.view(0, far), self.relay_l, self.right)
        self.far_l = self.post.send(self.view(1, far), self.relay_r, self.left)

    def start_near(self):
        self.near_r = self.post.send(self.view(1, up(self.me)), self.left_b, self.right)
        self.near_l = self.post.send(self.view(0, down(self.me)), self.right_a, self.left)

    def relay(self):
        self.far_r.wait_recv()
        self.add(0, up(self.me), [self.relay_l])
        self.last_r = self.post.send(self.view(0, up(self.me)), self.left_a, self.right)
        self.far_l.wait_recv()
        self.add(1, down(self.me), [self.relay_r])
        self.last_l = self.post.send(self.view(1, down(self.me)), self.right_b, self.left)

    def finish(self):
        self.near_r.wait_recv()
        self.near_l.wait_recv()
        self.last_r.wait_recv()
        self.add(0, self.me, [self.left_a, self.right_a])
        self.last_l.wait_recv()
        self.add(1, self.me, [self.left_b, self.right_b])


def sum_kernel(grads, small, out, small_out, mine, theirs, big, mid, low, acc, arrived, own_sems, send_sems, recv_sems):
    me = Place()
    greet(me.neighbours())
    post = Post(send_sems, recv_sems)
    x, y, z, zl, c, t = me.x, me.y, me.z, me.zl, me.c, me.t
    to_c = me.at(c=1 - c)
    rings = {
        "x": (x, me.at(x=up(x)), me.at(x=down(x))),
        "y": (y, me.at(y=up(y)), me.at(y=down(y))),
        "z": (z, me.at(z=up(z)), me.at(z=down(z))),
    }

    def side(d):
        return lax.rem(lax.div(d, 2) + t, 2)

    def chunk(ref, part, d):
        if part == 0:
            return ref.at[:, 0, d]
        if part == 1:
            return ref.at[:, 1, :, :, d]
        return ref.at[side(d), 2, :, lax.rem(d, 2)]

    def chunk_block(ref, part, k):
        if part == 0:
            return ref.at[lax.div(k, 8), lax.rem(lax.div(k, 4), 2), lax.rem(k, 4)]
        if part == 1:
            return ref.at[lax.div(k, 8), lax.rem(lax.div(k, 2), 4), lax.rem(k, 2)]
        return ref.at[lax.div(k, 4), lax.rem(k, 4)]

    partners = [
        to_c,
        me.at(x=x + 1 - 2 * lax.rem(x, 2)),
        me.at(x=3 - x),
        me.at(y=y + 1 - 2 * lax.rem(y, 2)),
        me.at(y=3 - y),
        me.at(z=z + 1 - 2 * lax.rem(z, 2)),
        me.at(z=3 - z),
    ]
    acc[0] = small[...]
    state = {"step": 0, "copy": None}

    def small_send():
        k = state["step"]
        state["copy"] = post.send(acc.at[k], arrived.at[k], partners[k])

    def small_next():
        k = state["step"]
        state["copy"].wait_recv()
        acc[k + 1] = acc[k] + arrived[k]
        state["step"] = k + 1
        if k + 1 < 7:
            small_send()

    small_send()

    kinds = [across, up, down, lambda v: v]
    order = [(part, kind) for kind in range(4) for part in range(3)]
    where = [x, y, z]
    core = {}
    for n, (part, kind) in enumerate(order):
        d = kinds[kind](where[part])
        src, dst = chunk(grads, part, d), chunk(theirs, part, d)
        if part == 0:
            there, here = src.at[..., 1 - c, :, :], src.at[..., c, :, :]
        else:
            there, here = src.at[..., 1 - c, :, :], src.at[..., c, :, :]
        local = pltpu.make_async_copy(here, chunk(mine, part, d), own_sems.at[n])
        local.start()
        core[part, kind] = (post.send(there, dst, to_c), local)

    def settle(part, kind):
        d = kinds[kind](where[part])
        remote, local = core[part, kind]
        local.wait()
        remote.wait_recv()
        target, source = chunk(mine, part, d), chunk(theirs, part, d)
        add_blocks(
            16,
            lambda k: chunk_block(target, part, k),
            [lambda k: chunk_block(source, part, k)],
        )

    def first_view(part):
        def view(half, d):
            ref = chunk(mine, part, d)
            if part == 2:
                return ref.at[pl.ds(2 * half, 2)]
            return ref.at[half]

        return view

    def first_block(part):
        if part == 0:
            return lambda ref, k: ref.at[lax.div(k, 4), lax.rem(k, 4)]
        if part == 1:
            return lambda ref, k: ref.at[lax.div(k, 2), lax.rem(k, 2)]
        return lambda ref, k: ref.at[lax.div(k, 4), lax.rem(k, 4)]

    def big_bufs(part):
        shapes = [(2, 4), (4, 2), (2, 4)]
        return [big[part].at[i] for i in range(6)]

    stage = [
        Ring(post, *rings["xyz"[part]], first_view(part), (8, 8), first_block(part), big_bufs(part))
        for part in range(3)
    ]
    for part in range(3):
        settle(part, 0)
        stage[part].start_far()
    small_next()
    for part in range(3):
        settle(part, 1)
        settle(part, 2)
        stage[part].start_near()
    small_next()
    for part in range(3):
        stage[part].relay()
    small_next()
    for part in range(3):
        settle(part, 3)

    def second_view(part):
        def view(half, d):
            if part == 0:
                return mine.at[half, 0, x, :, d]
            if part == 1:
                return mine.at[side(d), 1, pl.ds(2 * half, 2), lax.rem(d, 2), y]
            return mine.at[0, 2, d, zl, pl.ds(2 * half, 2)]

        return view

    second = []
    for part in range(3):
        stage[part].finish()
        ring = Ring(
            post,
            *rings["yzx"[part]],
            second_view(part),
            (2, 2),
            lambda ref, k: ref.at[k],
            [mid.at[part, i] for i in range(6)],
        )
        ring.start_far()
        ring.start_near()
        second.append(ring)
    small_next()
    for ring in second:
        ring.relay()
    small_next()

    def third_view(part):
        def view(half, d):
            rows = pl.ds(0, 32) if half == 0 else pl.ds(32, 16)
            if part == 0:
                return mine.at[side(d), 0, x, lax.rem(d, 2), y, rows]
            if part == 1:
                return mine.at[0, 1, d, zl, y, rows]
            return mine.at[0, 2, x, zl, d, rows]

        return view

    third = []
    for part in range(3):
        second[part].finish()
        bufs = [
            low.at[part, i, pl.ds(0, 32) if half == 0 else pl.ds(32, 16)]
            for i, half in enumerate((0, 1, 0, 1, 0, 1))
        ]
        ring = Ring(post, *rings["zxy"[part]], third_view(part), (None, None), None, bufs)
        ring.start_far()
        ring.start_near()
        third.append(ring)
    small_next()
    for ring in third:
        ring.relay()
    small_next()
    small_out[...] = acc[7]
    locals_ = []
    for part in range(3):
        third[part].finish()
        local = pltpu.make_async_copy(
            mine.at[0, part, x, zl, y], out.at[part, x, zl, y, c], own_sems.at[12 + part]
        )
        local.start()
        locals_.append(local)
    for local in locals_:
        local.wait()
    gather_blocks(me, post, out)
    post.drain()


SUM_COPIES = 7 + 12 + 3 * 3 * 6


def summed_grads(grads, small):
    count = GATHER_COPIES + SUM_COPIES
    block = (BLOCK, HALF)
    first_shapes = [(6, 2, 4), (6, 4, 2), (6, 2, 4)]

    def kernel(g, s, out, s_out, mine, theirs, big0, big1, big2, *rest):
        sum_kernel(g, s, out, s_out, mine, theirs, (big0, big1, big2), *rest)

    return pl.pallas_call(
        kernel,
        out_shape=(
            jax.ShapeDtypeStruct((3, 4, 2, 4, 2, *block), BF16),
            jax.ShapeDtypeStruct(small.shape, F32),
        ),
        in_specs=[ANY, VMEM],
        out_specs=(ANY, VMEM),
        scratch_shapes=[
            pltpu.VMEM((2, 3, 4, 2, 4, *block), BF16),
            pltpu.VMEM((2, 3, 4, 2, 4, *block), BF16),
            *[pltpu.VMEM((*shape, *block), BF16) for shape in first_shapes],
            pltpu.VMEM((3, 6, 2, *block), BF16),
            pltpu.VMEM((3, 6, *block), BF16),
            pltpu.VMEM((8, *small.shape), F32),
            pltpu.VMEM((7, *small.shape), F32),
            pltpu.SemaphoreType.DMA((15,)),
            pltpu.SemaphoreType.DMA((count,)),
            pltpu.SemaphoreType.DMA((count,)),
        ],
        compiler_params=pltpu.CompilerParams(
            collective_id=1, has_side_effects=True, vmem_limit_bytes=40 << 20
        ),
        name="gradient_sum",
    )(grads, small)


def dot(a, b, dims=((1,), (0,))):
    return lax.dot_general(a, b, (dims, ((), ())), preferred_element_type=F32)


NT = ((1,), (1,))
TN = ((0,), (0,))


def phi_terms(h):
    v = h * 0.7071067811865476
    v = jnp.clip(v, -3.7439211627767994, 3.7439211627767994)
    s = v * v
    top = 0.00022905065861350646
    for k in (0.0034082910107109506, 0.050955695062380861, 0.18520832239976145, 1.128379143519084):
        top = top * s + k
    low = -1.1791602954361697e-7
    for k in (
        0.000023547966471313185,
        0.0010179625278914885,
        0.014070470171167667,
        0.11098505178285362,
        0.49746925110067538,
        1.0,
    ):
        low = low * s + k
    big = 0.5 + 0.5 * (v * top / low)
    small = jnp.exp(h * h * -0.5) * 0.3989422804014327
    return big, big + h * small


def norm_stats(v):
    center = jnp.mean(v, axis=-1, keepdims=True)
    centered = v - center
    spread = jnp.mean(centered * centered, axis=-1, keepdims=True)
    scale = lax.rsqrt(spread + EPSILON)
    return centered * scale, scale


def row_loop(step, rows=16):
    def body(k, carry):
        step(pl.ds(pl.multiple_of(k * rows, rows), rows))
        return carry

    lax.fori_loop(0, BOTH // rows, body, 0)


def layer_kernel(
    counts,
    x_in,
    cot_in,
    vectors,
    small_mine,
    small_other,
    project,
    output,
    expand,
    reduce,
    other,
    block_out,
    input_grad,
    grads,
    small_out,
    w_qkv,
    w_out,
    w_expand,
    w_reduce,
    g_all,
    stream,
    resid,
    grad_resid,
    go,
    normed,
    normed_two,
    qkv,
    mixed,
    grad_mixed,
    probs,
    hidden,
    slope,
    active,
    grad_hidden,
    branch,
    dnorm,
    grad_attended,
    grad_qkv,
    sums,
    w_sems,
    g_sems,
):
    t = lax.axis_index("tensor")
    loads = []

    def load(src, dst):
        copy = pltpu.make_async_copy(src, dst, w_sems.at[len(loads)])
        copy.start()
        loads.append(copy)

    left, right = pl.ds(0, HALF), pl.ds(HALF, HALF)
    for j in range(3):
        load(project.at[j], w_qkv.at[j, :, left])
        load(other.at[0, pl.ds(j * WIDTH, WIDTH)], w_qkv.at[j, :, right])
    load(output, w_out.at[left])
    load(other.at[0, pl.ds(3 * WIDTH, HALF)], w_out.at[right, left])
    load(other.at[0, pl.ds(3 * WIDTH + HALF, HALF)], w_out.at[right, right])
    for j in range(2):
        load(expand.at[:, pl.ds(j * WIDTH, WIDTH)], w_expand.at[j])
        load(reduce.at[pl.ds(j * WIDTH, WIDTH)], w_reduce.at[j])
        for k, cols in enumerate((left, right)):
            load(other.at[1, pl.ds((2 * j + k) * WIDTH, WIDTH)], w_expand.at[2 + j, :, cols])
            load(
                other.at[2, pl.ds(k * 2 * WIDTH + j * WIDTH, WIDTH)],
                w_reduce.at[2 + j, :, cols],
            )

    stores = []

    def store(src, dst):
        copy = pltpu.make_async_copy(src, dst, g_sems.at[len(stores)])
        copy.start()
        stores.append(copy)

    live = counts[0] - 2 * t
    keep = [jnp.where(live > i, 1.0, 0.0) for i in range(2)]
    first_gain, first_shift = vectors[0:1], vectors[1:2]
    second_gain, second_shift = vectors[2:3], vectors[3:4]
    output_bias, reduce_bias = vectors[4:5], vectors[5:6]
    sums[...] = jnp.zeros_like(sums)

    def gather_sum(row, value):
        sums[pl.ds(row * 8, 8)] += value.reshape(-1, 8, WIDTH).sum(axis=0)

    def first_norm(rows):
        v = x_in[rows].astype(F32)
        n, _ = norm_stats(v)
        normed[rows] = (n * first_gain + first_shift).astype(BF16)

    row_loop(first_norm)
    for i in range(2):
        own = pl.ds(i * ROWS, ROWS)
        go[own] = (cot_in[own].astype(F32) * keep[i]).astype(BF16)

    for copy in loads[:6]:
        copy.wait()

    def project_step(j, carry):
        bias = jnp.concatenate([small_mine[pl.ds(j, 1)], small_other[pl.ds(j, 1)]], axis=1)
        result = (dot(normed[...], w_qkv[j]) + bias).astype(BF16)
        for p in range(PAIRS):
            qkv[j, p] = result[:, 128 * p : 128 * (p + 1)]
        return carry

    lax.fori_loop(0, 3, project_step, 0)

    lane = lax.broadcasted_iota(jnp.int32, (ROWS, 128), 1)
    first_head = lane < HD

    def split(pair):
        zero = jnp.zeros_like(pair)
        return jnp.concatenate(
            [jnp.where(first_head, pair, zero), jnp.where(first_head, zero, pair)], axis=0
        )

    def joined(both):
        return jnp.where(first_head, both[:ROWS], both[ROWS:])

    def image_rows(i):
        return pl.ds(pl.multiple_of(i * ROWS, 16), ROWS)

    key_dead = lax.broadcasted_iota(jnp.int32, (2 * ROWS, ROWS), 1) >= TOKENS

    def attend(k, carry):
        p, rows = lax.div(k, 2), image_rows(lax.rem(k, 2))
        queries = split(qkv[0, p, rows] * jnp.asarray(HD**-0.5, BF16))
        scores = dot(queries, qkv[1, p, rows], NT)
        scores = jnp.where(key_dead, -1e30, scores)
        raised = jnp.exp(scores - jnp.max(scores, axis=-1, keepdims=True))
        soft = raised / jnp.sum(raised, axis=-1, keepdims=True)
        probs[k] = soft
        mixed[p, rows] = joined(dot(soft.astype(BF16), qkv[2, p, rows])).astype(BF16)
        return carry

    lax.fori_loop(0, 2 * PAIRS, attend, 0)

    def all_pairs(ref):
        return jnp.concatenate([ref[p] for p in range(PAIRS)], axis=1)

    for copy in loads[6:9]:
        copy.wait()
    resid[...] = dot(all_pairs(mixed), w_out[...])

    def second_norm(rows):
        v = resid[rows] + x_in[rows].astype(F32) + output_bias
        resid[rows] = v
        n, _ = norm_stats(v)
        normed_two[rows] = (n * second_gain + second_shift).astype(BF16)

    row_loop(second_norm)

    for copy in loads[9:]:
        copy.wait()
    branch[...] = jnp.zeros_like(branch)
    dnorm[...] = jnp.zeros_like(dnorm)

    def feed(j, carry):
        o, jj = lax.div(j, 2), lax.rem(j, 2)
        at = 2 + 2 * jj
        bias_mine = jnp.concatenate([small_mine[pl.ds(at + 1, 1)], small_mine[pl.ds(at + 2, 1)]], axis=1)
        bias_other = jnp.concatenate([small_other[pl.ds(at + 1, 1)], small_other[pl.ds(at + 2, 1)]], axis=1)
        bias = jnp.where(o == 0, bias_mine, bias_other)
        hidden[...] = dot(normed_two[...], w_expand[j]) + bias

        def gelu(rows):
            h = hidden[rows]
            big, slope_rows = phi_terms(h)
            active[rows] = (h * big).astype(BF16)
            slope[rows] = slope_rows

        row_loop(gelu)
        branch[...] += dot(active[...], w_reduce[j])
        grad_active = dot(go[...], w_reduce[j], NT)
        gh = (grad_active * slope[...]).astype(BF16)
        grad_hidden[...] = gh
        sums[pl.ds(pl.multiple_of((8 + j) * 8, 8), 8)] = gh.astype(F32).reshape(-1, 8, WIDTH).sum(axis=0)
        dnorm[...] += dot(grad_hidden[...], w_expand[j], NT)
        grad = dot(normed_two[...], grad_hidden[...], TN).astype(BF16)
        start = pl.multiple_of(jj * 2 * WIDTH, WIDTH)
        g_all[o, 1, pl.ds(start, WIDTH)] = grad[:, :HALF]
        g_all[o, 1, pl.ds(start + WIDTH, WIDTH)] = grad[:, HALF:]
        grad = dot(active[...], go[...], TN).astype(BF16)
        start = pl.multiple_of(jj * WIDTH, WIDTH)
        g_all[o, 2, pl.ds(start, WIDTH)] = grad[:, :HALF]
        g_all[o, 2, pl.ds(start + 2 * WIDTH, WIDTH)] = grad[:, HALF:]
        return carry

    lax.fori_loop(0, 4, feed, 0)
    for o in range(2):
        store(g_all.at[o, pl.ds(1, 2)], grads.at[o, pl.ds(1, 2)])

    for i in range(2):
        own = pl.ds(i * ROWS, ROWS)
        block_out[own] = ((resid[own] + branch[own] + reduce_bias) * keep[i]).astype(BF16)

    def norm_back(n, scale, grad, gain):
        e = grad * gain
        return scale * (
            e - jnp.mean(e, axis=-1, keepdims=True) - n * jnp.mean(e * n, axis=-1, keepdims=True)
        )

    def second_back(rows):
        n, scale = norm_stats(resid[rows])
        grad = dnorm[rows]
        total = go[rows].astype(F32)
        gather_sum(5, total)
        total = total + norm_back(n, scale, grad, second_gain)
        grad_resid[rows] = total
        low = total.astype(BF16)
        grad_attended[rows] = low
        gather_sum(2, grad * n)
        gather_sum(3, grad)
        gather_sum(4, low.astype(F32))

    row_loop(second_back)

    grad = dot(all_pairs(mixed), grad_attended[...], TN).astype(BF16)
    for o in range(2):
        for k in range(2):
            g_all[o, 0, 3 * WIDTH + k * HALF : 3 * WIDTH + (k + 1) * HALF] = grad[
                o * HALF : (o + 1) * HALF, k * HALF : (k + 1) * HALF
            ]
    result = dot(grad_attended[...], w_out[...], NT).astype(BF16)
    for p in range(PAIRS):
        grad_mixed[p] = result[:, 128 * p : 128 * (p + 1)]

    def attend_back(k, carry):
        p, rows = lax.div(k, 2), image_rows(lax.rem(k, 2))
        grad_out = split(grad_mixed[p, rows])
        soft = probs[k]
        grad_soft = dot(grad_out, qkv[2, p, rows], NT)
        inner = jnp.sum(soft * grad_soft, axis=-1, keepdims=True)
        grad_scores = (soft * (grad_soft - inner)).astype(BF16)
        scale = jnp.asarray(HD**-0.5, BF16)
        queries = split(qkv[0, p, rows] * scale)
        grad_qkv[0, p, rows] = joined(dot(grad_scores, qkv[1, p, rows] * scale)).astype(BF16)
        grad_qkv[1, p, rows] = dot(grad_scores, queries, TN).astype(BF16)
        grad_qkv[2, p, rows] = dot(soft.astype(BF16), grad_out, TN).astype(BF16)
        return carry

    lax.fori_loop(0, 2 * PAIRS, attend_back, 0)

    dnorm[...] = jnp.zeros_like(dnorm)

    def project_back(j, carry):
        given = jnp.concatenate([grad_qkv[j, p] for p in range(PAIRS)], axis=1)
        grad = dot(normed[...], given, TN).astype(BF16)
        start = pl.multiple_of(j * WIDTH, WIDTH)
        g_all[0, 0, pl.ds(start, WIDTH)] = grad[:, :HALF]
        g_all[1, 0, pl.ds(start, WIDTH)] = grad[:, HALF:]
        dnorm[...] += dot(given, w_qkv[j], NT)
        part = given.astype(F32).reshape(-1, 8, WIDTH).sum(axis=0)
        row = jnp.where(j == 0, 6, jnp.where(j == 2, 7, 12))
        sums[pl.ds(pl.multiple_of(row * 8, 8), 8)] = part
        return carry

    lax.fori_loop(0, 3, project_back, 0)
    for o in range(2):
        store(g_all.at[o, 0], grads.at[o, 0])

    def first_back(rows):
        n, scale = norm_stats(x_in[rows].astype(F32))
        grad = dnorm[rows]
        input_grad[rows] = grad_resid[rows] + norm_back(n, scale, grad, first_gain)
        gather_sum(0, grad * n)
        gather_sum(1, grad)

    row_loop(first_back)

    totals = [jnp.sum(sums[8 * k : 8 * (k + 1)], axis=0, keepdims=True) for k in range(12)]
    first = t == 0

    def swapped(row):
        return jnp.where(first, row, jnp.concatenate([row[:, HALF:], row[:, :HALF]], axis=1))

    rows = totals[:6] + [swapped(totals[6]), swapped(totals[7])]
    for k in range(4):
        rows.append(jnp.where(first, totals[8 + k], totals[8 + (k + 2) % 4]))
    for k in range(12):
        small_out[k : k + 1] = rows[k]
    small_out[12:16] = jnp.zeros((4, WIDTH), F32)
    for copy in stores:
        copy.wait()


def layer(counts, x, cot, vectors, small_mine, small_other, weights, other):
    def buf(*shape, dtype=BF16):
        return pltpu.VMEM(shape, dtype)

    return pl.pallas_call(
        layer_kernel,
        out_shape=(
            jax.ShapeDtypeStruct((BOTH, WIDTH), BF16),
            jax.ShapeDtypeStruct((BOTH, WIDTH), F32),
            jax.ShapeDtypeStruct((2, 3, 4 * WIDTH, HALF), BF16),
            jax.ShapeDtypeStruct((16, WIDTH), F32),
        ),
        in_specs=[SMEM] + [VMEM] * 5 + [ANY] * 5,
        out_specs=(VMEM, VMEM, ANY, VMEM),
        scratch_shapes=[
            buf(3, WIDTH, WIDTH),
            buf(WIDTH, WIDTH),
            buf(4, WIDTH, WIDTH),
            buf(4, WIDTH, WIDTH),
            buf(2, 3, 4 * WIDTH, HALF),
            buf(8, 128, dtype=F32),
            buf(BOTH, WIDTH, dtype=F32),
            buf(BOTH, WIDTH, dtype=F32),
            buf(BOTH, WIDTH),
            buf(BOTH, WIDTH),
            buf(BOTH, WIDTH),
            buf(3, PAIRS, BOTH, 128),
            buf(PAIRS, BOTH, 128),
            buf(PAIRS, BOTH, 128),
            buf(2 * PAIRS, 2 * ROWS, ROWS, dtype=F32),
            buf(BOTH, WIDTH, dtype=F32),
            buf(BOTH, WIDTH, dtype=F32),
            buf(BOTH, WIDTH),
            buf(BOTH, WIDTH),
            buf(BOTH, WIDTH, dtype=F32),
            buf(BOTH, WIDTH, dtype=F32),
            buf(BOTH, WIDTH),
            buf(3, PAIRS, BOTH, 128),
            buf(13 * 8, WIDTH, dtype=F32),
            pltpu.SemaphoreType.DMA((24,)),
            pltpu.SemaphoreType.DMA((4,)),
        ],
        compiler_params=pltpu.CompilerParams(vmem_limit_bytes=62 << 20),
        name="layer",
    )(counts, x, cot, vectors, small_mine, small_other, *weights, other)


def shards(
    inputs,
    image_counts,
    first_gain,
    first_shift,
    project_weight,
    project_bias,
    output_weight,
    output_bias,
    second_gain,
    second_shift,
    expand_weight,
    expand_bias,
    reduce_weight,
    reduce_bias,
    out_cotangent,
):
    project = jnp.transpose(project_weight, (1, 0, 2))
    small = jnp.concatenate(
        [
            project_bias[0:1],
            jnp.zeros((1, HALF), F32),
            project_bias[1:2],
            expand_bias.reshape(4, HALF),
            jnp.zeros((1, HALF), F32),
        ]
    )
    weights = (project, output_weight, expand_weight, reduce_weight)
    other, small_other = other_weights(*weights, small)
    vectors = jnp.stack(
        [first_gain, first_shift, second_gain, second_shift, output_bias, reduce_bias, first_gain, first_gain]
    )

    def padded(array):
        return jnp.pad(array, ((0, 0), (0, ROWS - TOKENS), (0, 0))).reshape(BOTH, WIDTH)

    block_out, input_grad, grads, small_grads = layer(
        image_counts,
        padded(inputs),
        padded(out_cotangent),
        vectors,
        small,
        small_other,
        weights,
        other.reshape(3, 4 * WIDTH, HALF),
    )
    total, small_total = summed_grads(
        grads.reshape(2, 3, 4, 2, 4, 2, BLOCK, HALF), small_grads
    )
    total = total.reshape(3, 4 * WIDTH, HALF)
    t = lax.axis_index("tensor")

    def own_tokens(array):
        return array.reshape(2, ROWS, WIDTH)[:, :TOKENS]

    def side_by_side(array, count):
        rows = array.shape[0] // count
        return jnp.transpose(array.reshape(count, rows, HALF), (1, 0, 2)).reshape(
            rows, count * HALF
        )

    attention = total[0]
    project_grad = jnp.transpose(
        attention[: 3 * WIDTH].reshape(3, WIDTH, HALF), (1, 0, 2)
    ).astype(F32)
    output_grad = side_by_side(attention[3 * WIDTH :], 2).astype(F32)
    expand_grad = side_by_side(total[1], 4).astype(F32)
    reduce_grad = side_by_side(total[2], 2).astype(F32)
    project_bias_grad = lax.dynamic_slice(small_total, (6, t * HALF), (2, HALF))
    expand_bias_grad = lax.dynamic_slice(small_total, (8 + 2 * t, 0), (2, WIDTH)).reshape(-1)
    return (
        own_tokens(block_out),
        own_tokens(input_grad),
        small_total[0],
        small_total[1],
        project_grad,
        project_bias_grad,
        output_grad,
        small_total[4],
        small_total[2],
        small_total[3],
        expand_grad,
        expand_bias_grad,
        reduce_grad,
        small_total[5],
    )


def solution(mesh):
    in_specs = (
        P(("dp", "tensor"), None, None),
        P("dp"),
        P(),
        P(),
        P(None, None, "tensor"),
        P(None, "tensor"),
        P("tensor", None),
        P(),
        P(),
        P(),
        P(None, "tensor"),
        P("tensor"),
        P("tensor", None),
        P(),
        P(("dp", "tensor"), None, None),
    )
    out_specs = (
        P(("dp", "tensor"), None, None),
        P(("dp", "tensor"), None, None),
        P(),
        P(),
        P(None, None, "tensor"),
        P(None, "tensor"),
        P("tensor", None),
        P(),
        P(),
        P(),
        P(None, "tensor"),
        P("tensor"),
        P("tensor", None),
        P(),
    )
    return jax.shard_map(shards, mesh=mesh, in_specs=in_specs, out_specs=out_specs, check_vma=False)
```

time: 885 us -> 221 us (0.25); the launches traced: 875 us -> 221 us
  blocking collectives: 346 us -> 0 us
  waiting for transfers between devices: 254 us -> 0 us
  Pallas kernels: 0 us -> 190 us
  local copies, waits for them, and re-layouts: 109 us -> 26.2 us
  matrix products: 72.9 us -> 0 us
  starting transfers between devices: 38.3 us -> 0 us
  other arithmetic: 38.7 us -> 2.71 us
  between operations: 16 us -> 1.55 us
    psum x2 -> x0, blocking collectives: 346 us -> none  [the longest x1 275 us: shards(): lax.psum((grad_project_weight, grad_project_bias, grad_output_weight, gra...]
    psum x1 -> x0, waiting for transfers between devices: 190 us -> none  [shards(): lax.psum((grad_project_weight, grad_project_bias, grad_output_weight, gra...]
    pallas_call x0 -> x3, Pallas kernels: none -> 190 us  [the longest x1 73.2 us: layer(): pl.pallas_call(layer_kernel, out_shape=(jax.ShapeDtypeStruct((BOTH, WIDTH...]
    dot_general x22 -> x0, matrix products: 72.9 us -> none  [the longest x1 14.1 us: shards(): jnp.einsum('rd,fd->rf', grad_rows, reduce_weight, preferred_element_type=...]
    all_to_all x8 -> x0, waiting for transfers between devices: 63.8 us -> none  [the longest x1 24.5 us: sum_at_owner(): lax.all_to_all(blocks, axis, split_axis=0, concat_axis=0, tiled=True)]
    all_to_all x8 -> x0, starting transfers between devices: 38.2 us -> none  [the longest x4 19.2 us: copy_for_each(): lax.all_to_all(jnp.broadcast_to(shard[None], (length, *shard.shape)), axi...]
    reduce_sum x13 -> x0, other arithmetic: 25 us -> none  [the longest x6 10.5 us: layer_norm(): return centered * lax.rsqrt(spread + EPSILON) * gain + shift]
    unnamed x157 -> x28, local copies, waits for them, and re-layouts: 29.5 us -> 7.37 us
  transfers between devices with their start and end apart: 9 -> 0, of which waited for: 7 -> 0; matrix products, arithmetic and copies ran while one was open for 9% -> 0% of each run, Pallas kernels for 0% -> 0%
where the time goes in v1:
time: 221 us
  Pallas kernels  190 us (86%)
  local copies, waits for them, and re-layouts  26.2 us (12%)
  other arithmetic  2.71 us (1%)
    pallas_call x1, Pallas kernels, layer(): pl.pallas_call(layer_kernel, out_shape=(jax.ShapeDtypeStruct((BOTH, WIDTH...  73.2 us
    pallas_call x1, Pallas kernels, summed_grads(): pl.pallas_call(kernel, out_shape=(jax.ShapeDtypeStruct((3, 4, 2, 4, 2, *b...  72.3 us
    pallas_call x1, Pallas kernels, other_weights(): pl.pallas_call(weights_kernel, out_shape=(jax.ShapeDtypeStruct((3, 4, 2,...  44.6 us
    unnamed x28, local copies, waits for them, and re-layouts  7.37 us

profile of v1, /device:TPU:1, one launch (start us, length us, event | category | flops | bytes accessed | tf_op | source)
XLA Modules:
  0.0 220.7 jit_solution(9383229605012748637)
XLA Ops:
  0.6 0.8 fusion.1
  1.4 0.7 reshape.84
  2.1 0.6 concatenate.3.small.small_mine
  2.7 44.6 %weights_gather.1 = (bf16[3,4,2,4,2,48,384]{6,5,4,3,2,1,0:T(8,128)(2,1)}, f32[8,384]{1,0:T(8,128)}) custom-call(bf16[3,768,384]{2,1,0:T(8,128)(2,1)} %bitcast.34, bf16[384,768]{1,0:T(8,128)(2,1)} %output.3, bf16[768,1536]{1,0:T(8,128)(2,1)} %expand.3, bf16[1536,768]{1,0:T(8,128)(2,1)} %reduce.15, f32[8,384]{1,0:T(8,128)} %concatenate.3.small.small_mine), custom_call_target="tpu_custom_call" | custom-call | tf_op jit(solution)/shard_map/weights_gather/pallas_call | solution.py:232
  47.4 0.0 copy-start.4
  47.5 0.1 copy.38
  47.6 0.9 pad.7.clone
  48.4 0.0 copy-done.4
  48.5 0.1 copy.39
  48.5 0.9 pad.8.clone
  49.5 0.7 stack.29.vectors
  50.8 73.2 %layer.1 = (bf16[416,768]{1,0:T(8,128)(2,1)}, f32[416,768]{1,0:T(8,128)}, bf16[2,3,3072,384]{3,2,1,0:T(8,128)(2,1)}, f32[16,768]{1,0:T(8,128)}) custom-call(s32[1]{0:T(128)S(6)} %copy.43.counts, bf16[416,768]{1,0:T(8,128)(2,1)} %bitcast.38, bf16[416,768]{1,0:T(8,128)(2,1)} %bitcast.39, f32[8,768]{1,0:T(8,128)} %stack.29.vectors, ...), custom_call_target="tpu_custom_call" | custom-call | tf_op jit(solution)/shard_map/layer/pallas_call | solution.py:869
  124.0 0.8 copy-done.1
  124.8 72.3 %gradient_sum.1 = (bf16[3,4,2,4,2,48,384]{6,5,4,3,2,1,0:T(8,128)(2,1)S(1)}, f32[16,768]{1,0:T(8,128)S(1)}) custom-call(bf16[2,3,4,2,4,2,48,384]{7,6,5,4,3,2,1,0:T(8,128)(2,1)} %bitcast.29, f32[16,768]{1,0:T(8,128)S(1)} %copy-done.1), custom_call_target="tpu_custom_call" | custom-call | tf_op jit(solution)/shard_map/gradient_sum/pallas_call | solution.py:506
  197.2 2.9 %copy-done = bf16[3,4,2,4,2,48,384]{6,5,4,3,2,1,0:T(8,128)(2,1)} copy-done((bf16[3,4,2,4,2,48,384]{6,5,4,3,2,1,0:T(8,128)(2,1)}, bf16[3,4,2,4,2,48,384]{6,5,4,3,2,1,0:T(8,128)(2,1)S(1)}, u32[]{:S(2)}) %copy-start) | copy-done | bytes 7077912
  200.1 0.7 constant_dynamic-slice_fusion
  200.7 0.6 reshape.89
  201.3 0.6 slice_reduce_fusion
  202.0 3.0 %fusion = (bf16[1,4,2,4,2,48,384]{6,5,4,3,2,1,0:T(8,128)(2,1)S(1)}, bf16[1,4,2,4,2,48,384]{6,5,4,3,2,1,0:T(8,128)(2,1)S(1)}) fusion(bf16[3,4,2,4,2,48,384]{6,5,4,3,2,1,0:T(8,128)(2,1)} %copy-done), kind=kLoop, calls=%fused_computation.12 | loop fusion | bytes 9437184 | tf_op jit(solution)/shard_map/slice | solution.py:979
  205.0 0.3 convert_bitcast_fusion.1
  205.3 2.8 %copy.41 = f32[4,96,8,384]{3,2,0,1:T(8,128)} copy(f32[4,96,8,384]{3,2,1,0:T(8,128)S(1)} %convert_bitcast_fusion.1) | data formatting | bytes 9437184 | tf_op jit(solution)/shard_map/convert_element_type | solution.py:978
  208.1 0.3 convert_bitcast_fusion
  208.5 2.6 %copy.42 = f32[2,192,8,384]{3,2,0,1:T(8,128)} copy(f32[2,192,8,384]{3,2,1,0:T(8,128)S(1)} %convert_bitcast_fusion) | data formatting | bytes 9437184 | tf_op jit(solution)/shard_map/convert_element_type | solution.py:979
  211.0 1.7 slice.56
  212.7 2.0 convert_bitcast_fusion.2
  214.7 1.1 slice.57
  215.9 0.1 convert_bitcast_fusion.3
  215.9 1.1 copy.40
  217.0 0.5 copy-done.2
  217.6 0.1 slice.65
  217.7 1.6 copy.37
  219.4 1.3 copy.36
  (28 shorter events, 0.1 us)
Async XLA Ops:
  2.7 44.7 %copy-start.3 = (bf16[2,197,768]{2,0,1:T(2,128)(2,1)S(1)}, bf16[2,197,768]{2,0,1:T(2,128)(2,1)}, u32[]{:S(2)}) copy-start(bf16[2,197,768]{2,0,1:T(2,128)(2,1)} %param.15) | copy-start | bytes 1815556
  47.4 1.1 copy-start.4
  47.4 2.0 copy-start.6
  47.4 2.0 copy-start.7
  47.4 2.0 copy-start.8
  47.5 2.0 copy-start.9
  47.5 2.0 copy-start.10
  47.5 2.0 copy-start.11
  124.0 0.8 copy-start.1
  197.1 2.9 %copy-start = (bf16[3,4,2,4,2,48,384]{6,5,4,3,2,1,0:T(8,128)(2,1)}, bf16[3,4,2,4,2,48,384]{6,5,4,3,2,1,0:T(8,128)(2,1)S(1)}, u32[]{:S(2)}) copy-start(bf16[3,4,2,4,2,48,384]{6,5,4,3,2,1,0:T(8,128)(2,1)S(1)} %get-tuple-element.29) | copy-start | bytes 21233668
  215.8 1.7 copy-start.2
  217.6 1.7 copy-start.5

commit v2 on v0

v2 whole, which is shorter than its diff:
```python
import functools

import jax
import jax.numpy as jnp
from jax import lax
from jax.experimental import pallas as pl
from jax.experimental.pallas import tpu as pltpu
from jax.sharding import PartitionSpec as P

HD = 64
EPSILON = 1e-06
TOKENS = 197
ROWS = 208
BOTH = 2 * ROWS
WIDTH = 768
HALF = 384
PAIRS = 6
BLOCK = 48
THIRD = 16
MESH = pl.DeviceIdType.MESH
F32 = jnp.float32
BF16 = jnp.bfloat16
ANY = pl.BlockSpec(memory_space=pl.ANY)
VMEM = pl.BlockSpec(memory_space=pltpu.VMEM)
SMEM = pl.BlockSpec(memory_space=pltpu.SMEM)


class Place:
    def __init__(self):
        dp, t = lax.axis_index("dp"), lax.axis_index("tensor")
        self.dp, self.t = dp, t
        c, y = lax.rem(dp, 2), lax.rem(lax.div(dp, 2), 4)
        zl, x = lax.rem(lax.div(dp, 8), 2), lax.div(dp, 16)
        z = t * 2 + zl
        self.c, self.other_c = c, 1 - c
        self.zl, self.other_zl = zl, 1 - zl
        kinds = {"own": 0, "up": 1, "far": 2, "down": 3}
        self.x = {kind: lax.rem(x + step, 4) for kind, step in kinds.items()}
        self.y = {kind: lax.rem(y + step, 4) for kind, step in kinds.items()}
        depth = {kind: lax.rem(z + step, 4) for kind, step in kinds.items()}
        self.z_low = {kind: lax.rem(d, 2) for kind, d in depth.items()}
        self.side = {kind: lax.rem(lax.div(d, 2) + t, 2) for kind, d in depth.items()}

        def at(x, y, z, c):
            return (((x * 2 + lax.rem(z, 2)) * 4 + y) * 2 + c, lax.div(z, 2))

        self.to = {
            "x": tuple(at(self.x[kind], y, z, c) for kind in ("up", "down", "far")),
            "y": tuple(at(x, self.y[kind], z, c) for kind in ("up", "down", "far")),
            "z": tuple(at(x, y, depth[kind], c) for kind in ("up", "down", "far")),
        }
        self.to_core = at(x, y, z, 1 - c)
        self.to_low = at(x, y, t * 2 + 1 - zl, c)
        self.to_half = at(x, y, 3 - z, c)
        self.butterfly = [
            self.to_core,
            at(x + 1 - 2 * lax.rem(x, 2), y, z, c),
            at(3 - x, y, z, c),
            at(x, y + 1 - 2 * lax.rem(y, 2), z, c),
            at(x, 3 - y, z, c),
            at(x, y, z + 1 - 2 * lax.rem(z, 2), c),
            at(x, y, 3 - z, c),
        ]

    def greet(self):
        devices = [self.to_core, *self.to["x"], *self.to["y"], *self.to["z"]]
        barrier = pltpu.get_barrier_semaphore()
        for device in devices:
            pl.semaphore_signal(barrier, inc=1, device_id=device, device_id_type=MESH)
        pl.semaphore_wait(barrier, len(devices))


class Post:
    def __init__(self, send_sems, recv_sems):
        self.send_sems, self.recv_sems, self.copies = send_sems, recv_sems, []

    def describe(self, src, dst, device, k):
        return pltpu.make_async_remote_copy(
            src_ref=src,
            dst_ref=dst,
            send_sem=self.send_sems.at[k],
            recv_sem=self.recv_sems.at[k],
            device_id=device,
            device_id_type=MESH,
        )

    def send(self, src, dst, device):
        copy = self.describe(src, dst, device, len(self.copies))
        copy.start()
        self.copies.append(copy)
        return copy

    def drain(self):
        for copy in self.copies:
            copy.wait_send()


ALL = slice(None)
ATTENTION, FEED = 0, 1


def gather_steps(me, post, out, group):
    kinds = 0 if group == ATTENTION else pl.ds(1, 2)
    x, y, zl, zo, c = me.x, me.y, me.zl, me.other_zl, me.c
    (xr, xl, xf), (yr, yl, yf) = me.to["x"], me.to["y"]

    def view(third, at_x, at_zl, at_y):
        return out.at[kinds, at_x, at_zl, at_y, c, pl.ds(third * THIRD, THIRD)]

    def put(device, *spot):
        ref = view(*spot)
        return post.send(ref, ref, device)

    def share(*spot):
        cores.append(put(me.to_core, *spot))

    def wait(*copies):
        for copy in copies:
            copy.wait_recv()

    cores = []
    X, Y = x["own"], y["own"]
    a1 = put(me.to_low, 0, X, zl, Y)
    b1 = [put(device, 1, X, zl, Y) for device in (xr, xl, xf)]
    d1 = [put(device, 2, X, zl, Y) for device in (yr, yl, yf)]
    yield
    wait(a1)
    a2 = [put(device, 0, X, ALL, Y) for device in (yr, yl, yf)]
    wait(*d1)
    d2 = [put(device, 2, X, zl, ALL) for device in (xr, xl, xf)]
    wait(*b1)
    b2 = put(me.to_low, 1, ALL, zl, Y)
    d3 = [put(me.to_low, 2, X, zl, ALL)]
    share(2, X, zl, ALL)
    yield
    wait(*a2)
    a3r, a3l = put(xr, 0, X, ALL, ALL), put(xl, 0, X, ALL, ALL)
    wait(b2)
    b3r, b3l = put(yr, 1, ALL, ALL, Y), put(yl, 1, ALL, ALL, Y)
    wait(*d2)
    for kind in ("down", "up", "far"):
        d3.append(put(me.to_low, 2, x[kind], zl, ALL))
    share(0, X, ALL, ALL)
    share(1, ALL, ALL, Y)
    for kind in ("down", "up", "far"):
        share(2, x[kind], zl, ALL)
    yield
    wait(a3r)
    a3fr = put(xr, 0, x["down"], 0, ALL)
    wait(a3l)
    a3fl = put(xl, 0, x["up"], 1, ALL)
    wait(b3r)
    b3fr = put(yr, 1, ALL, 0, y["down"])
    wait(b3l)
    b3fl = put(yl, 1, ALL, 1, y["up"])
    share(0, x["down"], ALL, ALL)
    share(0, x["up"], ALL, ALL)
    share(1, ALL, ALL, y["down"])
    share(1, ALL, ALL, y["up"])
    for copy, kind in zip(d3[:2], ("own", "down")):
        wait(copy)
        share(2, x[kind], zo, ALL)
    yield
    for copy, kind in zip(d3[2:], ("up", "far")):
        wait(copy)
        share(2, x[kind], zo, ALL)
    wait(a3fr, a3fl)
    share(0, x["far"], ALL, ALL)
    wait(b3fr, b3fl)
    share(1, ALL, ALL, y["far"])
    yield
    wait(*cores)


GATHER_COPIES = 7 + 8 + 4 + 3 + 4 + 16


def other_weights_start(me, post, project, output, expand, reduce, weights):
    place = (me.x["own"], me.other_zl, me.y["own"], me.c)
    slots = [weights.at[(1, part, *place)] for part in range(3)]
    first = post.describe(slots[0], slots[0], me.to_half, 0)
    post.copies.append(first)
    column = [pl.multiple_of(k * HALF, HALF) for k in (me.x["own"], me.half_x, me.other_zl)]

    @pl.when(me.x["own"] < 3)
    def _():
        post.describe(project.at[place], slots[0], me.to_half, 0).start()

    @pl.when(me.x["own"] >= 3)
    def _():
        src = output.at[me.y["own"], me.c, :, pl.ds(column[2], HALF)]
        post.describe(src, slots[0], me.to_half, 0).start()

    src = expand.at[me.other_zl, me.y["own"], me.c, :, pl.ds(column[0], HALF)]
    second = post.send(src, slots[1], me.to_half)
    src = reduce.at[me.odd_x, me.other_zl, me.y["own"], me.c, :, pl.ds(column[1], HALF)]
    third = post.send(src, slots[2], me.to_half)
    return first, second, third


AXES = ("xyz", "yzx", "zxy")


def grad_view(grads, me, group, third, stage, half, kind):
    order = AXES[third]
    spot = {"o": ALL, "x": ALL, "zl": ALL, "y": ALL}
    for n, axis in enumerate(order[: stage + 1]):
        at = kind if n == stage else "own"
        if axis == "z":
            spot["o"], spot["zl"] = me.side[at], me.z_low[at]
        else:
            spot[axis] = getattr(me, axis)[at]
    if half is None:
        part = 0 if group == ATTENTION else pl.ds(1, 2)
    elif group == FEED:
        part = 1 + half
    else:
        part = 0
        left = order[stage + 1 :]
        if "z" in left:
            spot["o"] = half
        else:
            spot[left[0]] = pl.ds(2 * half, 2)
    rows = pl.ds(third * THIRD, THIRD)
    return grads.at[spot["o"], part, spot["x"], spot["zl"], spot["y"], me.c, rows]


HELD = (
    (((6, 2, 4), (6, 4, 2), (6, 2, 4)), ((3, 2, 2), (3, 4), (3, 4)), ((3,), (3,), (3,))),
    (
        ((6, 2, 2, 4), (6, 2, 4, 2), (6, 4, 4)),
        ((3, 2, 2, 2), (3, 2, 4), (3, 2, 4)),
        ((3, 2), (3, 2), (3, 2)),
    ),
)


def add_into(ref, bufs):
    total = ref[...].astype(F32)
    for buf in bufs:
        total = total + buf[...].astype(F32)
    ref[...] = total.astype(BF16)


class Direct:
    def __init__(self, me, post, grads, bufs, group, third, stage):
        self.view = lambda kind: grad_view(grads, me, group, third, stage, None, kind)
        self.bufs = [bufs.at[i] for i in range(3)]
        self.copies = [
            post.send(self.view(kind), buf, device)
            for kind, buf, device in zip(
                ("up", "down", "far"), self.bufs, me.to[AXES[third][stage]]
            )
        ]

    def finish(self):
        for copy in self.copies:
            copy.wait_recv()
        add_into(self.view("own"), self.bufs)


class Ring:
    def __init__(self, me, post, grads, bufs, group, third, stage):
        self.me, self.post, self.grads = me, post, grads
        self.key = (group, third, stage)
        self.right, self.left, _ = me.to[AXES[third][stage]]
        self.relay_l, self.relay_r, self.left_a, self.left_b, self.right_a, self.right_b = (
            bufs.at[i] for i in range(6)
        )

    def view(self, half, kind):
        group, third, stage = self.key
        return grad_view(self.grads, self.me, group, third, stage, half, kind)

    def add(self, half, kind, bufs):
        add_into(self.view(half, kind), bufs)

    def start(self):
        self.far_r = self.post.send(self.view(0, "far"), self.relay_l, self.right)
        self.far_l = self.post.send(self.view(1, "far"), self.relay_r, self.left)
        self.near_r = self.post.send(self.view(1, "up"), self.left_b, self.right)
        self.near_l = self.post.send(self.view(0, "down"), self.right_a, self.left)

    def relay(self):
        self.far_r.wait_recv()
        self.add(0, "up", [self.relay_l])
        self.last_r = self.post.send(self.view(0, "up"), self.left_a, self.right)
        self.far_l.wait_recv()
        self.add(1, "down", [self.relay_r])
        self.last_l = self.post.send(self.view(1, "down"), self.right_b, self.left)

    def finish(self):
        self.near_r.wait_recv()
        self.near_l.wait_recv()
        self.last_r.wait_recv()
        self.add(0, "own", [self.left_a, self.right_a])
        self.last_l.wait_recv()
        self.add(1, "own", [self.left_b, self.right_b])


def sum_steps(me, post, grads, theirs, bufs, out, own_sem, group):
    kinds = 0 if group == ATTENTION else pl.ds(1, 2)
    core = []
    if group == ATTENTION:
        for at in (3, 0, 1, 2):
            src = grads.at[:, 0, at, :, :, me.other_c]
            core.append(post.send(src, theirs.at[:, 0, at], me.to_core))
            yield
        for at, copy in zip((3, 0, 1, 2), core):
            copy.wait_recv()

            def step(o, carry, at=at):
                add_into(grads.at[o, 0, at, :, :, me.c], [theirs.at[o, 0, at]])
                return carry

            lax.fori_loop(0, 2, step, 0)
    else:
        for o in range(2):
            src = grads.at[o, kinds, :, :, :, me.other_c]
            core.append(post.send(src, theirs.at[o, kinds], me.to_core))
            yield
        for o in range(2):
            core[o].wait_recv()

            def step(k, carry, o=o):
                part, at = 1 + lax.div(k, 4), lax.rem(k, 4)
                add_into(grads.at[o, part, at, :, :, me.c], [theirs.at[o, part, at]])
                return carry

            lax.fori_loop(0, 8, step, 0)
            if o == 0:
                yield
    rings = [Ring(me, post, grads, bufs[0][third], group, third, 0) for third in range(3)]
    for ring in rings:
        ring.start()
    yield
    for ring in rings:
        ring.relay()
    yield
    for stage in range(1, 3):
        lines = []
        for third, ring in enumerate(rings):
            ring.finish()
            lines.append(Direct(me, post, grads, bufs[stage][third], group, third, stage))
        rings = lines
        yield
    for ring in rings:
        ring.finish()
    X, Y = me.x["own"], me.y["own"]
    local = pltpu.make_async_copy(
        grads.at[0, kinds, X, me.zl, Y, me.c], out.at[kinds, X, me.zl, Y, me.c], own_sem
    )
    local.start()
    local.wait()
    yield from gather_steps(me, post, out, group)


def small_steps(me, post, acc, arrived):
    for k, partner in enumerate(me.butterfly):
        copy = post.send(acc.at[k], arrived.at[k], partner)
        yield
        copy.wait_recv()
        acc[k + 1] = acc[k] + arrived[k]


COPIES = 4 + 4 * GATHER_COPIES + 6 + 2 * 3 * (6 + 3 + 3) + 7


def dot(a, b, dims=((1,), (0,))):
    return lax.dot_general(a, b, (dims, ((), ())), preferred_element_type=F32)


NT = ((1,), (1,))
TN = ((0,), (0,))


def phi_terms(h):
    v = h * 0.7071067811865476
    v = jnp.clip(v, -3.7439211627767994, 3.7439211627767994)
    s = v * v
    top = 0.00022905065861350646
    for k in (0.0034082910107109506, 0.050955695062380861, 0.18520832239976145, 1.128379143519084):
        top = top * s + k
    low = -1.1791602954361697e-7
    for k in (
        0.000023547966471313185,
        0.0010179625278914885,
        0.014070470171167667,
        0.11098505178285362,
        0.49746925110067538,
        1.0,
    ):
        low = low * s + k
    big = 0.5 + 0.5 * (v * top / low)
    small = jnp.exp(h * h * -0.5) * 0.3989422804014327
    return big, big + h * small


def norm_stats(v):
    center = jnp.mean(v, axis=-1, keepdims=True)
    centered = v - center
    spread = jnp.mean(centered * centered, axis=-1, keepdims=True)
    scale = lax.rsqrt(spread + EPSILON)
    return centered * scale, scale


def row_loop(step, rows=16, start=0, stop=BOTH):
    def body(k, carry):
        step(pl.ds(pl.multiple_of(k * rows, rows), rows))
        return carry

    lax.fori_loop(start // rows, stop // rows, body, 0)


def poke(*steps):
    for step in steps:
        next(step, None)


def finish(*steps):
    for step in steps:
        for _ in step:
            pass


def layer_kernel(
    counts,
    x_in,
    cot_in,
    vectors,
    small_mine,
    project,
    output,
    expand,
    reduce,
    block_out,
    input_grad,
    total_out,
    small_out,
    weights,
    grads,
    theirs,
    *rest,
):
    bufs = [[rest[9 * g + 3 * s : 9 * g + 3 * s + 3] for s in range(3)] for g in range(2)]
    (
        small_other,
        acc,
        arrived,
        block_low,
        resid,
        grad_resid,
        go,
        normed,
        normed_two,
        qkv,
        mixed,
        grad_mixed,
        probs,
        hidden,
        active,
        grad_hidden,
        branch,
        dnorm,
        grad_attended,
        grad_qkv,
        sums,
        w_sems,
        own_sems,
        send_sems,
        recv_sems,
    ) = rest[18:]
    me = Place()
    me.half_x, me.odd_x = lax.div(me.x["own"], 2), lax.rem(me.x["own"], 2)
    t = me.t
    first = t == 0
    loads = []

    def load(src, dst):
        copy = pltpu.make_async_copy(src, dst, w_sems.at[len(loads)])
        copy.start()
        loads.append(copy)

    cols = [pl.ds(k * HALF, HALF) for k in range(4)]
    for j in range(3):
        load(project.at[j], weights.at[0, 0, j])
    for k in range(2):
        load(output.at[:, :, :, cols[k]], weights.at[0, 0, 3, k])
    for k in range(4):
        load(expand.at[:, :, :, :, cols[k]], weights.at[0, 1, k])
    for k in range(4):
        load(reduce.at[k % 2, :, :, :, :, cols[k // 2]], weights.at[0, 2, k])

    me.greet()
    post = Post(send_sems, recv_sems)
    pieces = other_weights_start(me, post, project, output, expand, reduce, weights)
    small_copy = post.send(small_mine, small_other, me.to_half)

    def weight_steps(group):
        yield
        for piece in pieces[:1] if group == ATTENTION else pieces[1:]:
            piece.wait_recv()
        yield from gather_steps(me, post, weights.at[1], group)

    wa, wf = weight_steps(ATTENTION), weight_steps(FEED)
    poke(wa, wf)

    live = counts[0] - 2 * t
    keep = [jnp.where(live > i, 1.0, 0.0) for i in range(2)]
    first_gain, first_shift = vectors[0:1], vectors[1:2]
    second_gain, second_shift = vectors[2:3], vectors[3:4]
    output_bias, reduce_bias = vectors[4:5], vectors[5:6]
    sums[...] = jnp.zeros_like(sums)

    def gather_sum(row, value):
        sums[pl.ds(row * 8, 8)] += value.reshape(-1, 8, WIDTH).sum(axis=0)

    def first_norm(rows):
        v = x_in[rows].astype(F32)
        n, _ = norm_stats(v)
        normed[rows] = (n * first_gain + first_shift).astype(BF16)

    row_loop(first_norm, 16, 0, ROWS)
    poke(wa)
    row_loop(first_norm, 16, ROWS, BOTH)
    poke(wa)
    for i in range(2):
        own = pl.ds(i * ROWS, ROWS)
        go[own] = (cot_in[own].astype(F32) * keep[i]).astype(BF16)

    lane = lax.broadcasted_iota(jnp.int32, (ROWS, 128), 1)
    first_head = lane < HD

    def split(pair):
        zero = jnp.zeros_like(pair)
        return jnp.concatenate(
            [jnp.where(first_head, pair, zero), jnp.where(first_head, zero, pair)], axis=0
        )

    def joined(both):
        return jnp.where(first_head, both[:ROWS], both[ROWS:])

    def image_rows(i):
        return pl.ds(pl.multiple_of(i * ROWS, 16), ROWS)

    def slab(o, part, at):
        return weights[o, part, at].reshape(WIDTH, HALF)

    def beside(*blocks):
        return jnp.concatenate(blocks, axis=1)

    key_dead = lax.broadcasted_iota(jnp.int32, (2 * ROWS, ROWS), 1) >= TOKENS

    def attend(k, carry):
        p, rows = lax.div(k, 2), image_rows(lax.rem(k, 2))
        queries = split(qkv[0, p, rows] * jnp.asarray(HD**-0.5, BF16))
        scores = dot(queries, qkv[1, p, rows], NT)
        scores = jnp.where(key_dead, -1e30, scores)
        raised = jnp.exp(scores - jnp.max(scores, axis=-1, keepdims=True))
        soft = (raised / jnp.sum(raised, axis=-1, keepdims=True)).astype(BF16)
        probs[k] = soft
        mixed[p, rows] = joined(dot(soft, qkv[2, p, rows])).astype(BF16)
        return carry

    for o in range(2):
        if o == 0:
            for copy in loads[:3]:
                copy.wait()
        else:
            finish(wa)
            small_copy.wait_recv()
        small = small_mine if o == 0 else small_other
        for j in range(3):
            result = (dot(normed[...], slab(o, 0, j)) + small[j : j + 1]).astype(BF16)
            for p in range(3):
                qkv[j, 3 * o + p] = result[:, 128 * p : 128 * (p + 1)]
            poke(wa, *([wf] if j == 2 or o == 1 else []))
        for k in range(0, 6, 2):
            lax.fori_loop(6 * o + k, 6 * o + k + 2, attend, 0)
            poke(wa, wf)

    def all_pairs(ref):
        return jnp.concatenate([ref[p] for p in range(PAIRS)], axis=1)

    for copy in loads[3:5]:
        copy.wait()

    def output_matrix():
        return jnp.concatenate(
            [
                beside(*(weights[o, 0, 3, k].reshape(HALF, HALF) for k in range(2)))
                for o in range(2)
            ],
            axis=0,
        )

    resid[...] = dot(all_pairs(mixed), output_matrix())
    poke(wf)

    def second_norm(rows):
        v = resid[rows] + x_in[rows].astype(F32) + output_bias
        resid[rows] = v
        n, _ = norm_stats(v)
        normed_two[rows] = (n * second_gain + second_shift).astype(BF16)

    row_loop(second_norm)
    poke(wf)

    for copy in loads[5:]:
        copy.wait()
    branch[...] = jnp.zeros_like(branch)
    dnorm[...] = jnp.zeros_like(dnorm)

    def feed(o, jj):
        small = small_mine if o == 0 else small_other
        bias = beside(small[pl.ds(3 + 2 * jj, 1)], small[pl.ds(4 + 2 * jj, 1)])
        w_expand = beside(slab(o, 1, 2 * jj), slab(o, 1, 2 * jj + 1))
        hidden[...] = dot(normed_two[...], w_expand) + bias

        def gelu(rows):
            h = hidden[rows]
            big, slope_rows = phi_terms(h)
            active[rows] = (h * big).astype(BF16)
            hidden[rows] = slope_rows

        row_loop(gelu)
        w_reduce = beside(slab(o, 2, jj), slab(o, 2, 2 + jj))
        branch[...] += dot(active[...], w_reduce)
        gh = (dot(go[...], w_reduce, NT) * hidden[...]).astype(BF16)
        grad_hidden[...] = gh
        row = (8 + 2 * o + jj) * 8
        sums[pl.ds(row, 8)] = gh.astype(F32).reshape(-1, 8, WIDTH).sum(axis=0)
        dnorm[...] += dot(grad_hidden[...], w_expand, NT)
        grad = dot(normed_two[...], grad_hidden[...], TN).astype(BF16)
        grads[o, 1, 2 * jj] = grad[:, :HALF].reshape(2, 4, 2, BLOCK, HALF)
        grads[o, 1, 2 * jj + 1] = grad[:, HALF:].reshape(2, 4, 2, BLOCK, HALF)
        grad = dot(active[...], go[...], TN).astype(BF16)
        grads[o, 2, jj] = grad[:, :HALF].reshape(2, 4, 2, BLOCK, HALF)
        grads[o, 2, 2 + jj] = grad[:, HALF:].reshape(2, 4, 2, BLOCK, HALF)

    sf = sum_steps(me, post, grads, theirs, bufs[1], total_out, own_sems.at[0], FEED)
    for jj in range(2):
        feed(0, jj)
        poke(wf)
    finish(wf)
    poke(sf)
    for jj in range(2):
        feed(1, jj)
    poke(sf)

    for i in range(2):
        own = pl.ds(i * ROWS, ROWS)
        block_low[own] = ((resid[own] + branch[own] + reduce_bias) * keep[i]).astype(BF16)
    block_store = pltpu.make_async_copy(block_low, block_out, own_sems.at[2])
    block_store.start()

    def norm_back(n, scale, grad, gain):
        e = grad * gain
        return scale * (
            e - jnp.mean(e, axis=-1, keepdims=True) - n * jnp.mean(e * n, axis=-1, keepdims=True)
        )

    def second_back(rows):
        n, scale = norm_stats(resid[rows])
        grad = dnorm[rows]
        total = go[rows].astype(F32)
        gather_sum(5, total)
        total = total + norm_back(n, scale, grad, second_gain)
        grad_resid[rows] = total
        low = total.astype(BF16)
        grad_attended[rows] = low
        gather_sum(2, grad * n)
        gather_sum(3, grad)
        gather_sum(4, low.astype(F32))

    row_loop(second_back)
    poke(sf)

    grad = dot(all_pairs(mixed), grad_attended[...], TN).astype(BF16)
    for o in range(2):
        for k in range(2):
            grads[o, 0, 3, k] = grad[
                o * HALF : (o + 1) * HALF, k * HALF : (k + 1) * HALF
            ].reshape(4, 2, BLOCK, HALF)
    sa = sum_steps(me, post, grads, theirs, bufs[0], total_out, own_sems.at[1], ATTENTION)
    poke(sa, sf)
    result = dot(grad_attended[...], output_matrix(), NT).astype(BF16)
    for p in range(PAIRS):
        grad_mixed[p] = result[:, 128 * p : 128 * (p + 1)]

    def attend_back(k, carry):
        p, rows = lax.div(k, 2), image_rows(lax.rem(k, 2))
        grad_out = split(grad_mixed[p, rows])
        soft_low = probs[k]
        soft = soft_low.astype(F32)
        grad_soft = dot(grad_out, qkv[2, p, rows], NT)
        inner = jnp.sum(soft * grad_soft, axis=-1, keepdims=True)
        grad_scores = (soft * (grad_soft - inner)).astype(BF16)
        scale = jnp.asarray(HD**-0.5, BF16)
        queries = split(qkv[0, p, rows] * scale)
        grad_qkv[0, p, rows] = joined(dot(grad_scores, qkv[1, p, rows] * scale)).astype(BF16)
        grad_qkv[1, p, rows] = dot(grad_scores, queries, TN).astype(BF16)
        grad_qkv[2, p, rows] = dot(soft_low, grad_out, TN).astype(BF16)
        return carry

    for k in range(0, 12, 6):
        lax.fori_loop(k, k + 6, attend_back, 0)
        poke(sf)

    for j in range(3):
        grad = dot(normed[...], all_pairs(grad_qkv.at[j]), TN).astype(BF16)
        for o in range(2):
            grads[o, 0, j] = grad[:, o * HALF : (o + 1) * HALF].reshape(2, 4, 2, BLOCK, HALF)
        poke(sa)
    poke(sf)
    for j in range(3):
        given = all_pairs(grad_qkv.at[j])
        back = dot(given, beside(slab(0, 0, j), slab(1, 0, j)), NT)
        if j == 0:
            dnorm[...] = back
        else:
            dnorm[...] += back
        if j != 1:
            row = 48 if j == 0 else 56
            sums[row : row + 8] = given.astype(F32).reshape(-1, 8, WIDTH).sum(axis=0)
        poke(sa, sf)

    def first_back(rows):
        n, scale = norm_stats(x_in[rows].astype(F32))
        grad = dnorm[rows]
        grad_resid[rows] = grad_resid[rows] + norm_back(n, scale, grad, first_gain)
        gather_sum(0, grad * n)
        gather_sum(1, grad)

    row_loop(first_back, 16, 0, ROWS)
    poke(sa, sf)
    row_loop(first_back, 16, ROWS, BOTH)
    input_store = pltpu.make_async_copy(grad_resid, input_grad, own_sems.at[3])
    input_store.start()

    totals = [jnp.sum(sums[8 * k : 8 * (k + 1)], axis=0, keepdims=True) for k in range(12)]

    def swapped(row):
        return jnp.where(first, row, jnp.concatenate([row[:, HALF:], row[:, :HALF]], axis=1))

    rows = totals[:6] + [swapped(totals[6]), swapped(totals[7])]
    for k in range(4):
        rows.append(jnp.where(first, totals[8 + k], totals[8 + (k + 2) % 4]))
    for k in range(12):
        acc[0, k : k + 1] = rows[k]
    acc[0, 12:16] = jnp.zeros((4, WIDTH), F32)
    sm = small_steps(me, post, acc, arrived)
    for _ in range(16):
        poke(sa, sm, sf)
    finish(sf, sm, sa)
    small_out[...] = acc[7]
    post.drain()
    block_store.wait()
    input_store.wait()


def layer(counts, x, cot, vectors, small, project, output, expand, reduce):
    def buf(*shape, dtype=BF16):
        return pltpu.VMEM(shape, dtype)

    ring_bufs = [
        buf(*HELD[group][stage][third], THIRD, HALF)
        for group in range(2)
        for stage in range(3)
        for third in range(3)
    ]
    blocks = (3, 4, 2, 4, 2, BLOCK, HALF)
    return pl.pallas_call(
        layer_kernel,
        out_shape=(
            jax.ShapeDtypeStruct((BOTH, WIDTH), BF16),
            jax.ShapeDtypeStruct((BOTH, WIDTH), F32),
            jax.ShapeDtypeStruct(blocks, BF16),
            jax.ShapeDtypeStruct((16, WIDTH), F32),
        ),
        in_specs=[SMEM] + [VMEM] * 4 + [ANY] * 4,
        out_specs=(ANY, ANY, ANY, VMEM),
        scratch_shapes=[
            buf(2, *blocks),
            buf(2, *blocks),
            buf(2, 3, 4, 2, 4, BLOCK, HALF),
            *ring_bufs,
            buf(*small.shape, dtype=F32),
            buf(8, 16, WIDTH, dtype=F32),
            buf(7, 16, WIDTH, dtype=F32),
            buf(BOTH, WIDTH),
            buf(BOTH, WIDTH, dtype=F32),
            buf(BOTH, WIDTH, dtype=F32),
            buf(BOTH, WIDTH),
            buf(BOTH, WIDTH),
            buf(BOTH, WIDTH),
            buf(3, PAIRS, BOTH, 128),
            buf(PAIRS, BOTH, 128),
            buf(PAIRS, BOTH, 128),
            buf(2 * PAIRS, 2 * ROWS, ROWS),
            buf(BOTH, WIDTH, dtype=F32),
            buf(BOTH, WIDTH),
            buf(BOTH, WIDTH),
            buf(BOTH, WIDTH, dtype=F32),
            buf(BOTH, WIDTH, dtype=F32),
            buf(BOTH, WIDTH),
            buf(3, PAIRS, BOTH, 128),
            buf(12 * 8, WIDTH, dtype=F32),
            pltpu.SemaphoreType.DMA((13,)),
            pltpu.SemaphoreType.DMA((4,)),
            pltpu.SemaphoreType.DMA((COPIES,)),
            pltpu.SemaphoreType.DMA((COPIES,)),
        ],
        compiler_params=pltpu.CompilerParams(
            collective_id=0, has_side_effects=True, vmem_limit_bytes=63 << 20
        ),
        name="layer",
    )(counts, x, cot, vectors, small, project, output, expand, reduce)


def shards(
    inputs,
    image_counts,
    first_gain,
    first_shift,
    project_weight,
    project_bias,
    output_weight,
    output_bias,
    second_gain,
    second_shift,
    expand_weight,
    expand_bias,
    reduce_weight,
    reduce_bias,
    out_cotangent,
):
    small = jnp.concatenate(
        [
            project_bias[0:1],
            jnp.zeros((1, HALF), F32),
            project_bias[1:2],
            expand_bias.reshape(4, HALF),
            jnp.zeros((1, HALF), F32),
        ]
    )
    vectors = jnp.stack(
        [first_gain, first_shift, second_gain, second_shift, output_bias, reduce_bias, first_gain, first_gain]
    )

    def padded(array):
        return jnp.pad(array, ((0, 0), (0, ROWS - TOKENS), (0, 0))).reshape(BOTH, WIDTH)

    block_out, input_grad, total, small_total = layer(
        image_counts,
        padded(inputs),
        padded(out_cotangent),
        vectors,
        small,
        jnp.transpose(project_weight, (1, 0, 2)).reshape(3, 2, 4, 2, BLOCK, HALF),
        output_weight.reshape(4, 2, BLOCK, WIDTH),
        expand_weight.reshape(2, 4, 2, BLOCK, 4 * HALF),
        reduce_weight.reshape(2, 2, 4, 2, BLOCK, WIDTH),
    )
    total = total.reshape(3, 4 * WIDTH, HALF)
    t = lax.axis_index("tensor")

    def own_tokens(array):
        return array.reshape(2, ROWS, WIDTH)[:, :TOKENS]

    def side_by_side(array, count):
        rows = array.shape[0] // count
        return jnp.transpose(array.reshape(count, rows, HALF), (1, 0, 2)).reshape(
            rows, count * HALF
        )

    attention = total[0]
    project_grad = jnp.transpose(
        attention[: 3 * WIDTH].reshape(3, WIDTH, HALF), (1, 0, 2)
    ).astype(F32)
    output_grad = side_by_side(attention[3 * WIDTH :], 2).astype(F32)
    expand_grad = side_by_side(total[1], 4).astype(F32)
    reduce_grad = side_by_side(total[2], 2).astype(F32)
    project_bias_grad = lax.dynamic_slice(small_total, (6, t * HALF), (2, HALF))
    expand_bias_grad = lax.dynamic_slice(small_total, (8 + 2 * t, 0), (2, WIDTH)).reshape(-1)
    return (
        own_tokens(block_out),
        own_tokens(input_grad),
        small_total[0],
        small_total[1],
        project_grad,
        project_bias_grad,
        output_grad,
        small_total[4],
        small_total[2],
        small_total[3],
        expand_grad,
        expand_bias_grad,
        reduce_grad,
        small_total[5],
    )


def solution(mesh):
    in_specs = (
        P(("dp", "tensor"), None, None),
        P("dp"),
        P(),
        P(),
        P(None, None, "tensor"),
        P(None, "tensor"),
        P("tensor", None),
        P(),
        P(),
        P(),
        P(None, "tensor"),
        P("tensor"),
        P("tensor", None),
        P(),
        P(("dp", "tensor"), None, None),
    )
    out_specs = (
        P(("dp", "tensor"), None, None),
        P(("dp", "tensor"), None, None),
        P(),
        P(),
        P(None, None, "tensor"),
        P(None, "tensor"),
        P("tensor", None),
        P(),
        P(),
        P(),
        P(None, "tensor"),
        P("tensor"),
        P("tensor", None),
        P(),
    )
    return jax.shard_map(shards, mesh=mesh, in_specs=in_specs, out_specs=out_specs, check_vma=False)
```

time: 885 us -> 201 us (0.23)
  blocking collectives: 346 us -> 0 us
  waiting for transfers between devices: 254 us -> 0 us
  Pallas kernels: 0 us -> 167 us
  local copies, waits for them, and re-layouts: 109 us -> 26.3 us
  matrix products: 72.9 us -> 0 us
  starting transfers between devices: 38.3 us -> 0 us
  other arithmetic: 38.7 us -> 2.71 us
  between operations: 16 us -> 1.48 us
    psum x2 -> x0, blocking collectives: 346 us -> none  [the longest x1 275 us: shards(): lax.psum((grad_project_weight, grad_project_bias, grad_output_weight, gra...]
    psum x1 -> x0, waiting for transfers between devices: 190 us -> none  [shards(): lax.psum((grad_project_weight, grad_project_bias, grad_output_weight, gra...]
    pallas_call x0 -> x1, Pallas kernels: none -> 167 us  [layer(): pl.pallas_call(layer_kernel, out_shape=(jax.ShapeDtypeStruct((BOTH, WIDTH...]
    dot_general x22 -> x0, matrix products: 72.9 us -> none  [the longest x1 14.1 us: shards(): jnp.einsum('rd,fd->rf', grad_rows, reduce_weight, preferred_element_type=...]
    all_to_all x8 -> x0, waiting for transfers between devices: 63.8 us -> none  [the longest x1 24.5 us: sum_at_owner(): lax.all_to_all(blocks, axis, split_axis=0, concat_axis=0, tiled=True)]
    all_to_all x8 -> x0, starting transfers between devices: 38.2 us -> none  [the longest x4 19.2 us: copy_for_each(): lax.all_to_all(jnp.broadcast_to(shard[None], (length, *shard.shape)), axi...]
    unnamed x157 -> x14, local copies, waits for them, and re-layouts: 29.5 us -> 4.15 us
    reduce_sum x13 -> x0, other arithmetic: 25 us -> none  [the longest x6 10.5 us: layer_norm(): return centered * lax.rsqrt(spread + EPSILON) * gain + shift]
  transfers between devices with their start and end apart: 9 -> 0, of which waited for: 7 -> 0; matrix products, arithmetic and copies ran while one was open for 9% -> 0% of each run, Pallas kernels for 0% -> 0%
where the time goes in v2:
time: 201 us; the launch traced here: 198 us
  Pallas kernels  167 us (83%)
  local copies, waits for them, and re-layouts  26.3 us (13%)
  other arithmetic  2.71 us (1%)
    pallas_call x1, Pallas kernels, layer(): pl.pallas_call(layer_kernel, out_shape=(jax.ShapeDtypeStruct((BOTH, WIDTH...  167 us
    another operation x7, local copies, waits for them, and re-layouts, shards(): jnp.stack([first_gain, first_shift, second_gain, second_shift, output_bia...  4.78 us
    unnamed x14, local copies, waits for them, and re-layouts  4.15 us

profile of v2, /device:TPU:1, one launch (start us, length us, event | category | flops | bytes accessed | tf_op | source)
XLA Modules:
  0.0 197.7 jit_solution(15210733411969117944)
XLA Ops:
  1.4 0.7 stack.23
  2.1 0.7 stack.24
  2.8 0.7 stack.27
  3.4 0.7 stack.25
  4.1 0.7 stack.26
  4.8 0.7 stack.28
  5.5 0.8 fusion.1
  6.3 0.6 stack.29.vectors
  6.9 0.7 reshape.90
  7.6 0.6 concatenate.3.small_mine
  8.3 1.1 copy.38
  9.4 0.9 pad.7.clone
  10.3 0.1 copy.39
  10.3 0.9 pad.8.clone
  11.2 167.2 %layer.1 = (bf16[416,768]{1,0:T(8,128)(2,1)}, f32[416,768]{1,0:T(8,128)}, bf16[3,4,2,4,2,48,384]{6,5,4,3,2,1,0:T(8,128)(2,1)}, f32[16,768]{1,0:T(8,128)}) custom-call(s32[1]{0:T(128)S(6)} %copy.43.counts, bf16[416,768]{1,0:T(8,128)(2,1)} %bitcast.39, bf16[416,768]{1,0:T(8,128)(2,1)} %bitcast.40, f32[8,768]{1,0:T(8,128)} %stack.29.vectors, ...), custom_call_target="tpu_custom_call" | custom-call | tf_op jit(solution)/shard_map/layer/pallas_call | solution.py:773
  178.4 1.2 slice.64
  179.6 1.3 copy.36
  180.9 0.1 slice.65
  181.0 1.6 copy.37
  182.6 0.7 constant_dynamic-slice_fusion
  183.3 0.6 slice_reduce_fusion
  184.0 0.6 reshape.97
  184.6 1.1 slice.57
  185.7 0.1 convert_bitcast_fusion.3
  185.8 1.1 copy.40
  186.9 2.2 %slice.56 = bf16[1,3,2,4,2,48,384]{6,5,4,3,2,1,0:T(8,128)(2,1)S(1)} slice(bf16[3,4,2,4,2,48,384]{6,5,4,3,2,1,0:T(8,128)(2,1)} %get-tuple-element.21), slice={[0:1], [0:3], [0:2], [0:4], [0:2], [0:48], [0:384]} | slice | bytes 3538944 | tf_op jit(solution)/shard_map/slice | solution.py:879
  189.1 0.6 fusion
  189.7 2.0 %convert_bitcast_fusion.2 = f32[768,3,384]{2,0,1:T(8,128)} fusion(bf16[3,768,384]{2,1,0:T(8,128)(2,1)S(1)} %bitcast.36), kind=kLoop, calls=%fused_computation.2 | loop fusion | flops 884736 | bytes 5308416 | tf_op jit(solution)/shard_map/convert_element_type | solution.py:880
  191.7 0.3 convert_bitcast_fusion.1
  192.0 2.8 %copy.41 = f32[4,96,8,384]{3,2,0,1:T(8,128)} copy(f32[4,96,8,384]{3,2,1,0:T(8,128)S(1)} %convert_bitcast_fusion.1) | data formatting | bytes 9437184 | tf_op jit(solution)/shard_map/convert_element_type | solution.py:882
  194.8 0.3 convert_bitcast_fusion
  195.1 2.6 %copy.42 = f32[2,192,8,384]{3,2,0,1:T(8,128)} copy(f32[2,192,8,384]{3,2,1,0:T(8,128)S(1)} %convert_bitcast_fusion) | data formatting | bytes 9437184 | tf_op jit(solution)/shard_map/convert_element_type | solution.py:883
  (13 shorter events, 0.0 us)
Async XLA Ops:
  0.6 9.6 %copy-start.1 = (bf16[2,197,768]{2,0,1:T(2,128)(2,1)S(1)}, bf16[2,197,768]{2,0,1:T(2,128)(2,1)}, u32[]{:S(2)}) copy-start(bf16[2,197,768]{2,0,1:T(2,128)(2,1)} %param.29) | copy-start | bytes 1815556
  178.4 2.5 %copy-start = (f32[416,768]{1,0:T(8,128)S(1)}, f32[416,768]{1,0:T(8,128)}, u32[]{:S(2)}) copy-start(f32[416,768]{1,0:T(8,128)} %get-tuple-element.19) | copy-start | bytes 3833860
  180.9 1.7 copy-start.2
  180.9 8.1 %slice-start = ((s8[7077888]{0:T(1024)(128)(4,1)}), s8[2883584]{0:T(1024)(128)(4,1)S(1)}, s32[]{:S(2)}) async-start(s8[7077888]{0:T(1024)(128)(4,1)} %bitcast.34), calls=%async_computation | async-start | bytes 5767168
  185.7 3.4 %slice-start.1 = ((s8[7077888]{0:T(1024)(128)(4,1)}), s8[4194304]{0:T(1024)(128)(4,1)S(1)}, s32[]{:S(2)}) async-start(s8[7077888]{0:T(1024)(128)(4,1)} %bitcast.34), calls=%async_computation.1 | async-start | bytes 8388608
